TPU v7x, 32 devices: a whole 2x2x4 slice. The times are simulated.
32 devices in a mesh: dp: 2 (over core), ctx: 16 (over z, y, x).
Axes of the slice: x: 2, y: 2, z: 4, core: 2. Of those that a mesh axis runs over, the one named last changes fastest.
Arguments:
- hidden_in: bfloat16 [4, 2048, 1024], P('dp', 'ctx'), may hold values from -6 to 6
- segments: int32 [4, 2048], P('dp'), may hold values from 0 to 10, as said below
- routes: int32 [4, 2048, 8], P('dp', 'ctx'), may hold values from 0 to 31, all different within a row; in each aligned block of 128 rows (0 to 127, 128 to 255, ..., all dimensions but the last counted through in order) at most 40 rows name the same one
- grad_out: bfloat16 [4, 2048, 1024], P('dp', 'ctx'), may hold values from -6 to 6
- gain_attn: bfloat16 [1024], P(('dp', 'ctx')), may hold values from 0.5 to 1.5
- w_query: bfloat16 [1024, 1024], P(('dp', 'ctx')), may hold values from -0.1875 to 0.1875
- w_key: bfloat16 [1024, 512], P(('dp', 'ctx')), may hold values from -0.1875 to 0.1875
- w_value: bfloat16 [1024, 512], P(('dp', 'ctx')), may hold values from -0.1875 to 0.1875
- w_out: bfloat16 [1024, 1024], P(('dp', 'ctx')), may hold values from -3 to 3
- gain_moe: bfloat16 [1024], P(('dp', 'ctx')), may hold values from 0.5 to 1.5
- w_router: bfloat16 [1024, 32], P(('dp', 'ctx')), may hold values from -0.09375 to 0.09375
- w_in: bfloat16 [32, 1024, 1024], P('ctx', 'dp'), may hold values from -0.1875 to 0.1875
- w_down: bfloat16 [32, 512, 1024], P('ctx', None, 'dp'), may hold values from -1 to 1
Outputs:
- output_hidden: bfloat16 [4, 2048, 1024], P('dp', 'ctx')
- grad_hidden: float32 [4, 2048, 1024], P('dp', 'ctx')
- grad_gain_attn: float32 [1024], P(('dp', 'ctx'))
- grad_query: float32 [1024, 1024], P(('dp', 'ctx'))
- grad_key: float32 [1024, 512], P(('dp', 'ctx'))
- grad_value: float32 [1024, 512], P(('dp', 'ctx'))
- grad_out_proj: float32 [1024, 1024], P(('dp', 'ctx'))
- grad_gain_moe: float32 [1024], P(('dp', 'ctx'))
- grad_router: float32 [1024, 32], P(('dp', 'ctx'))
- grad_in: float32 [32, 1024, 1024], P('ctx', 'dp')
- grad_down: float32 [32, 512, 1024], P('ctx', None, 'dp')
Inputs may be any that keep to these rules, and one draw needn't show every extreme that they name: `segments`: segment numbers never fall along a sequence. Of sequences 2i and 2i + 1, one (drawn) is a single document numbered 2048 // 200; the other packs documents of 200 to 2000 positions numbered from 0, the last one possibly shorter. `routes`: each row names 8 different experts. In the 128 positions of one device of one sequence (aligned blocks), no expert is named more than 40 times.
All inputs are finite; a program needn't handle non-finite values.
Results may differ from a plain program's by a relative error of at most 0.024.
Values may be sent and summed in bfloat16 or wider, within the bound.
A program may use at most 192 MiB of HBM per device.

v0:
```python
import math

import jax
import jax.numpy as jnp
from jax import lax
from jax.sharding import PartitionSpec as P

HEADS = 16
KV_HEADS = 8
HEAD_DIM = 64


EPS = 1e-06
ROPE_BASE = 10000.0
NEG = -1e30


def rope_tables(positions, head_dim):
    steps_f = jnp.arange(0, head_dim, 2, dtype=jnp.float32)
    inv_freq = jnp.exp(-math.log(ROPE_BASE) * steps_f / head_dim)
    angle = positions.astype(jnp.float32)[:, None] * inv_freq[None, :]
    cosine = jnp.concatenate([jnp.cos(angle), jnp.cos(angle)], -1)[:, None, :]
    sine_table = jnp.concatenate([jnp.sin(angle), jnp.sin(angle)], -1)[:, None, :]
    return (cosine, sine_table)


def rotate(tensor, cosine, sine_table):
    half = tensor.shape[-1] // 2
    turned = jnp.concatenate([-tensor[..., half:], tensor[..., :half]], -1)
    return tensor * cosine + turned * sine_table


def rotate_back(gradient, cosine, sine_table):
    half = gradient.shape[-1] // 2
    scaled = gradient * sine_table
    turned = jnp.concatenate([scaled[..., half:], -scaled[..., :half]], -1)
    return gradient * cosine + turned


def norm_back(gradient, normed, inverse, gain_vec):
    scaled = gradient * gain_vec
    return inverse * (scaled - normed * jnp.mean(scaled * normed, -1, keepdims=True))


def split_blocks(pieces):
    amount = pieces[0].shape[0]
    block_size = math.gcd(amount, 512)
    number = amount // block_size
    split_parts = tuple((piece.reshape((number, block_size) + piece.shape[1:]) for piece in pieces))
    starts = jnp.arange(number, dtype=jnp.int32) * block_size
    return (split_parts, starts, block_size)


def block_mask(key_start, block_size, query_pos, query_seg, seg_row):
    key_pos = key_start + jnp.arange(block_size, dtype=jnp.int32)
    key_seg = lax.dynamic_slice_in_dim(seg_row, key_start, block_size)
    return (key_pos[None, :] <= query_pos[:, None]) & (key_seg[None, :] == query_seg[:, None])


def attend_forward(carried, pieces, queries, query_pos, query_seg, seg_row, score_scale):
    kv_heads = queries.shape[1]
    head_dim = queries.shape[3]
    split_parts, starts, block_size = split_blocks(pieces)

    def one_block(run_state, block_inputs):
        run_max, run_sum, run_acc = run_state
        key_block, value_block, key_start = block_inputs
        key_heads = key_block.reshape(block_size, kv_heads, head_dim)
        value_heads = value_block.reshape(block_size, kv_heads, head_dim)
        allowed = block_mask(key_start, block_size, query_pos, query_seg, seg_row)
        scores = (
            jnp.einsum("qhgd,khd->hgqk", queries, key_heads, preferred_element_type=jnp.float32)
            * score_scale
        )
        new_max = jnp.maximum(run_max, jnp.max(jnp.where(allowed, scores, NEG), -1))
        factor = jnp.exp(run_max - new_max)
        weights_exp = jnp.where(allowed, jnp.exp(scores - new_max[..., None]), 0.0)
        run_sum = run_sum * factor + jnp.sum(weights_exp, -1)
        run_acc = run_acc * factor[..., None] + jnp.einsum(
            "hgqk,khd->hgqd",
            weights_exp.astype(jnp.bfloat16),
            value_heads,
            preferred_element_type=jnp.float32,
        )
        return ((new_max, run_sum, run_acc), None)

    final_state, unused = lax.scan(one_block, carried, (split_parts[0], split_parts[1], starts))
    return final_state


def attend_backward(
    carried,
    pieces,
    queries,
    query_pos,
    query_seg,
    seg_row,
    score_scale,
    grad_heads,
    log_sum,
    delta_rows,
):
    grad_query, grad_keys, grad_values = carried
    kv_heads = queries.shape[1]
    head_dim = queries.shape[3]
    split_parts, starts, block_size = split_blocks(pieces)

    def one_block(grad_acc, block_inputs):
        key_block, value_block, key_start = block_inputs
        key_heads = key_block.reshape(block_size, kv_heads, head_dim)
        value_heads = value_block.reshape(block_size, kv_heads, head_dim)
        allowed = block_mask(key_start, block_size, query_pos, query_seg, seg_row)
        scores = (
            jnp.einsum("qhgd,khd->hgqk", queries, key_heads, preferred_element_type=jnp.float32)
            * score_scale
        )
        probs_full = jnp.where(allowed, jnp.exp(scores - log_sum[..., None]), 0.0)
        grad_value = jnp.einsum(
            "hgqk,qhgd->khd",
            probs_full.astype(jnp.bfloat16),
            grad_heads,
            preferred_element_type=jnp.float32,
        )
        grad_prob = jnp.einsum(
            "qhgd,khd->hgqk", grad_heads, value_heads, preferred_element_type=jnp.float32
        )
        grad_score = (probs_full * (grad_prob - delta_rows[..., None])).astype(jnp.bfloat16)
        grad_acc = (
            grad_acc
            + jnp.einsum(
                "hgqk,khd->hgqd", grad_score, key_heads, preferred_element_type=jnp.float32
            )
            * score_scale
        )
        grad_key = (
            jnp.einsum("hgqk,qhgd->khd", grad_score, queries, preferred_element_type=jnp.float32)
            * score_scale
        )
        return (grad_acc, (grad_key.reshape(block_size, -1), grad_value.reshape(block_size, -1)))

    grad_query, (key_parts, value_parts) = lax.scan(
        one_block, grad_query, (split_parts[0], split_parts[1], starts)
    )
    kv_width = grad_keys.shape[1]
    grad_keys = key_parts.reshape(-1, kv_width)
    grad_values = value_parts.reshape(-1, kv_width)
    return (grad_query, grad_keys, grad_values)


def on_device(
    hidden_in,
    segments,
    routes,
    grad_out,
    gain_attn,
    w_query,
    w_key,
    w_value,
    w_out,
    gain_moe,
    w_router,
    w_in,
    w_down,
):
    span_len = hidden_in.shape[1]
    model_width = hidden_in.shape[2]
    ctx_size = lax.axis_size("ctx")
    my_index = lax.axis_index("ctx")
    exp_dev = w_in.shape[0]
    experts = exp_dev * ctx_size
    hidden = w_down.shape[1]
    top_count = routes.shape[2]
    capacity = span_len * top_count * 5 // (4 * experts)
    kv_heads = KV_HEADS
    head_dim = HEAD_DIM
    groups = HEADS // KV_HEADS
    kv_width = kv_heads * head_dim
    seq_len = segments.shape[1]
    score_scale = head_dim ** (-0.5)
    query_pos = my_index * span_len + jnp.arange(span_len, dtype=jnp.int32)
    cosine, sine_table = rope_tables(query_pos, head_dim)
    assigns = span_len * top_count
    expert_ids = jnp.arange(experts, dtype=jnp.int32)
    f32 = jnp.float32
    bf16 = jnp.bfloat16

    def gather_layer(shards):
        return (
            lax.all_gather(shards[0], ("dp", "ctx"), axis=0, tiled=True),
            lax.all_gather(shards[1], ("dp", "ctx"), axis=0, tiled=True),
            lax.all_gather(shards[2], ("dp", "ctx"), axis=0, tiled=True),
            lax.all_gather(shards[3], ("dp", "ctx"), axis=0, tiled=True),
            lax.all_gather(shards[4], ("dp", "ctx"), axis=0, tiled=True),
            lax.all_gather(shards[5], ("dp", "ctx"), axis=0, tiled=True),
            lax.all_gather(shards[6], ("dp", "ctx"), axis=0, tiled=True),
        )

    def gather_expert(shards):
        return (
            lax.all_gather(shards[0], "dp", axis=1, tiled=True),
            lax.all_gather(shards[1], "dp", axis=2, tiled=True),
        )

    layer_shards = (gain_attn, w_query, w_key, w_value, w_out, gain_moe, w_router)
    expert_shards = (w_in, w_down)
    acc_gain_one = jnp.zeros((model_width,), f32)
    acc_query = jnp.zeros((model_width, w_query.shape[1]), f32)
    acc_key = jnp.zeros((model_width, kv_width), f32)
    acc_value = jnp.zeros((model_width, kv_width), f32)
    acc_proj = jnp.zeros((model_width, w_out.shape[1]), f32)
    acc_gain_two = jnp.zeros((model_width,), f32)
    acc_router = jnp.zeros((model_width, experts), f32)
    acc_in = jnp.zeros((exp_dev, model_width, 2 * hidden), f32)
    acc_down = jnp.zeros((exp_dev, hidden, model_width), f32)
    outputs = []
    input_grads = []
    for micro_step in range(hidden_in.shape[0]):
        gain_one, query_full, key_full, value_full, proj_full, gain_two, router_full = gather_layer(
            layer_shards
        )
        in_full, down_full = gather_expert(expert_shards)
        inputs = hidden_in[micro_step].astype(f32)
        inverse_one = lax.rsqrt(jnp.mean(inputs * inputs, -1, keepdims=True) + EPS)
        normed_one = inputs * inverse_one
        act_in = (normed_one * gain_one.astype(f32)).astype(bf16)
        query_raw = jnp.dot(act_in, query_full, preferred_element_type=f32)
        key_raw = jnp.dot(act_in, key_full, preferred_element_type=f32)
        values_low = jnp.dot(act_in, value_full, preferred_element_type=f32).astype(bf16)
        queries = rotate(query_raw.reshape(span_len, HEADS, head_dim), cosine, sine_table).astype(
            bf16
        )
        queries = queries.reshape(span_len, kv_heads, groups, head_dim)
        keys_low = (
            rotate(key_raw.reshape(span_len, kv_heads, head_dim), cosine, sine_table)
            .astype(bf16)
            .reshape(span_len, kv_width)
        )
        seg_row = segments[micro_step]
        query_seg = lax.dynamic_slice_in_dim(seg_row, my_index * span_len, span_len)
        start_state = (
            jnp.full((kv_heads, groups, span_len), NEG, f32),
            jnp.zeros((kv_heads, groups, span_len), f32),
            jnp.zeros((kv_heads, groups, span_len, head_dim), f32),
        )
        run_max, run_sum, run_acc = attend_forward(
            start_state,
            (
                lax.all_gather(keys_low, "ctx", axis=0, tiled=True),
                lax.all_gather(values_low, "ctx", axis=0, tiled=True),
            ),
            queries,
            query_pos,
            query_seg,
            seg_row,
            score_scale,
        )
        attn_heads = run_acc / run_sum[..., None]
        log_sum = run_max + jnp.log(run_sum)
        attn_rows = attn_heads.transpose(2, 0, 1, 3).reshape(span_len, HEADS * head_dim)
        attn_low = attn_rows.astype(bf16)
        resid = inputs + jnp.einsum("th,dh->td", attn_low, proj_full, preferred_element_type=f32)
        inverse_two = lax.rsqrt(jnp.mean(resid * resid, -1, keepdims=True) + EPS)
        normed_two = resid * inverse_two
        moe_in = (normed_two * gain_two.astype(f32)).astype(bf16)
        logits = jnp.dot(moe_in, router_full, preferred_element_type=f32)
        route_rows = routes[micro_step]
        chosen = (route_rows[:, :, None] == expert_ids).astype(f32)
        selected = jnp.sum(chosen * logits[:, None, :], -1)
        gate_weights = jax.nn.softmax(selected, -1)
        flat_routes = route_rows.reshape(assigns)
        member = (flat_routes[:, None] == expert_ids).astype(jnp.int32)
        rank_index = jnp.sum(member * (jnp.cumsum(member, 0) - 1), -1)
        slot_index = flat_routes * capacity + rank_index
        sources = (
            jnp.full((experts * capacity,), assigns, jnp.int32)
            .at[slot_index]
            .set(jnp.arange(assigns, dtype=jnp.int32))
        )
        token_src = sources // top_count
        padded_in = jnp.concatenate([moe_in, jnp.zeros((1, model_width), bf16)], 0)
        sent_rows = padded_in[token_src].reshape(ctx_size, exp_dev, capacity, model_width)
        mixed_pre = jnp.einsum(
            "sepd,edf->sepf",
            lax.all_to_all(sent_rows, "ctx", split_axis=0, concat_axis=0, tiled=True),
            in_full,
            preferred_element_type=f32,
        )
        product = (jax.nn.silu(mixed_pre[..., :hidden]) * mixed_pre[..., hidden:]).astype(bf16)
        result = jnp.einsum(
            "sepf,efd->sepd", product, down_full, preferred_element_type=f32
        ).astype(bf16)
        returned = lax.all_to_all(result, "ctx", split_axis=0, concat_axis=0, tiled=True)
        y_slots = returned.reshape(experts * capacity, model_width)
        y_tokens = y_slots[slot_index].reshape(span_len, top_count, model_width)
        moe_out = jnp.sum(gate_weights[:, :, None] * y_tokens, 1)
        outputs.append((resid + moe_out).astype(bf16))
        tied = lax.optimization_barrier((layer_shards, expert_shards, moe_out))
        gain_one, query_full, key_full, value_full, proj_full, gain_two, router_full = gather_layer(
            tied[0]
        )
        in_full, down_full = gather_expert(tied[1])
        grad_final = grad_out[micro_step].astype(f32)
        grad_y = (gate_weights[:, :, None] * grad_final[:, None, :]).astype(bf16)
        grad_gate = jnp.sum(grad_final[:, None, :] * y_tokens, -1)
        grad_sel = gate_weights * (grad_gate - jnp.sum(gate_weights * grad_gate, -1, keepdims=True))
        grad_logit = jnp.sum(grad_sel[:, :, None] * chosen, 1).astype(bf16)
        acc_router = acc_router + jnp.einsum(
            "td,te->de", moe_in, grad_logit, preferred_element_type=f32
        )
        grad_moe_in = jnp.einsum("te,de->td", grad_logit, router_full, preferred_element_type=f32)
        padded_grad = jnp.concatenate(
            [grad_y.reshape(assigns, model_width), jnp.zeros((1, model_width), bf16)], 0
        )
        grad_rows = padded_grad[sources].reshape(ctx_size, exp_dev, capacity, model_width)
        recv_rows, recv_grads = (
            lax.all_to_all(sent_rows, "ctx", split_axis=0, concat_axis=0, tiled=True),
            lax.all_to_all(grad_rows, "ctx", split_axis=0, concat_axis=0, tiled=True),
        )
        mixed_pre = jnp.einsum("sepd,edf->sepf", recv_rows, in_full, preferred_element_type=f32)
        gate_part = mixed_pre[..., :hidden]
        up_part = mixed_pre[..., hidden:]
        sigmoid_gate = jax.nn.sigmoid(gate_part)
        swish_gate = gate_part * sigmoid_gate
        product = (swish_gate * up_part).astype(bf16)
        grad_prod = jnp.einsum("sepd,efd->sepf", recv_grads, down_full, preferred_element_type=f32)
        grad_mixed = jnp.concatenate(
            [
                grad_prod * up_part * sigmoid_gate * (1.0 + gate_part * (1.0 - sigmoid_gate)),
                grad_prod * swish_gate,
            ],
            -1,
        ).astype(bf16)
        acc_down = acc_down + jnp.einsum(
            "sepf,sepd->efd", product, recv_grads, preferred_element_type=f32
        )
        acc_in = acc_in + jnp.einsum(
            "sepd,sepf->edf", recv_rows, grad_mixed, preferred_element_type=f32
        )
        grad_rows_in = jnp.einsum(
            "sepf,edf->sepd", grad_mixed, in_full, preferred_element_type=f32
        ).astype(bf16)
        grad_back = lax.all_to_all(
            grad_rows_in, "ctx", split_axis=0, concat_axis=0, tiled=True
        ).reshape(experts * capacity, model_width)
        grad_moe_in = grad_moe_in + jnp.sum(
            grad_back[slot_index].reshape(span_len, top_count, model_width), 1, dtype=f32
        )
        acc_gain_two = acc_gain_two + jnp.sum(grad_moe_in * normed_two, 0)
        grad_resid = grad_final + norm_back(
            grad_moe_in, normed_two, inverse_two, gain_two.astype(f32)
        )
        grad_attn_in = grad_resid.astype(bf16)
        acc_proj = acc_proj + jnp.einsum(
            "td,th->dh", grad_attn_in, attn_low, preferred_element_type=f32
        )
        grad_attn_low = jnp.dot(grad_attn_in, proj_full, preferred_element_type=f32).astype(bf16)
        grad_heads = grad_attn_low.reshape(span_len, kv_heads, groups, head_dim)
        delta_rows = jnp.sum(
            (grad_attn_low * attn_rows).reshape(span_len, kv_heads, groups, head_dim), -1
        ).transpose(1, 2, 0)
        back_state = (
            jnp.zeros((kv_heads, groups, span_len, head_dim), f32),
            jnp.zeros((seq_len, kv_width), f32),
            jnp.zeros((seq_len, kv_width), f32),
        )
        grad_query, grad_keys, grad_values = attend_backward(
            back_state,
            (
                lax.all_gather(keys_low, "ctx", axis=0, tiled=True),
                lax.all_gather(values_low, "ctx", axis=0, tiled=True),
            ),
            queries,
            query_pos,
            query_seg,
            seg_row,
            score_scale,
            grad_heads,
            log_sum,
            delta_rows,
        )
        key_grad, value_grad = (
            lax.psum_scatter(
                grad_keys.astype(jnp.bfloat16), "ctx", scatter_dimension=0, tiled=True
            ).astype(jnp.float32),
            lax.psum_scatter(
                grad_values.astype(jnp.bfloat16), "ctx", scatter_dimension=0, tiled=True
            ).astype(jnp.float32),
        )
        query_turn = grad_query.transpose(2, 0, 1, 3).reshape(span_len, HEADS, head_dim)
        grad_q_raw = (
            rotate_back(query_turn, cosine, sine_table)
            .reshape(span_len, HEADS * head_dim)
            .astype(bf16)
        )
        grad_k_raw = (
            rotate_back(key_grad.reshape(span_len, kv_heads, head_dim), cosine, sine_table)
            .reshape(span_len, kv_width)
            .astype(bf16)
        )
        grad_v_low = value_grad.astype(bf16)
        acc_query = acc_query + jnp.einsum(
            "td,th->dh", act_in, grad_q_raw, preferred_element_type=f32
        )
        acc_key = acc_key + jnp.einsum("td,th->dh", act_in, grad_k_raw, preferred_element_type=f32)
        acc_value = acc_value + jnp.einsum(
            "td,th->dh", act_in, grad_v_low, preferred_element_type=f32
        )
        grad_act = jnp.einsum("th,dh->td", grad_q_raw, query_full, preferred_element_type=f32)
        grad_act = grad_act + jnp.einsum(
            "th,dh->td", grad_k_raw, key_full, preferred_element_type=f32
        )
        grad_act = grad_act + jnp.einsum(
            "th,dh->td", grad_v_low, value_full, preferred_element_type=f32
        )
        acc_gain_one = acc_gain_one + jnp.sum(grad_act * normed_one, 0)
        input_grads.append(
            grad_resid + norm_back(grad_act, normed_one, inverse_one, gain_one.astype(f32))
        )
    layer_grads = (
        lax.psum_scatter(acc_gain_one, ("dp", "ctx"), scatter_dimension=0, tiled=True),
        lax.psum_scatter(acc_query, ("dp", "ctx"), scatter_dimension=0, tiled=True),
        lax.psum_scatter(acc_key, ("dp", "ctx"), scatter_dimension=0, tiled=True),
        lax.psum_scatter(acc_value, ("dp", "ctx"), scatter_dimension=0, tiled=True),
        lax.psum_scatter(acc_proj, ("dp", "ctx"), scatter_dimension=0, tiled=True),
        lax.psum_scatter(acc_gain_two, ("dp", "ctx"), scatter_dimension=0, tiled=True),
        lax.psum_scatter(acc_router, ("dp", "ctx"), scatter_dimension=0, tiled=True),
    )
    expert_grads = (
        lax.psum_scatter(acc_in.astype(jnp.bfloat16), "dp", scatter_dimension=1, tiled=True).astype(
            jnp.float32
        ),
        lax.psum_scatter(
            acc_down.astype(jnp.bfloat16), "dp", scatter_dimension=2, tiled=True
        ).astype(jnp.float32),
    )
    return (
        jnp.stack(outputs),
        jnp.stack(input_grads),
        layer_grads[0],
        layer_grads[1],
        layer_grads[2],
        layer_grads[3],
        layer_grads[4],
        layer_grads[5],
        layer_grads[6],
        expert_grads[0],
        expert_grads[1],
    )


def solution(mesh):
    placed = (
        P("dp", "ctx", None),
        P("dp", None),
        P("dp", "ctx", None),
        P("dp", "ctx", None),
        P(("dp", "ctx")),
        P(("dp", "ctx"), None),
        P(("dp", "ctx"), None),
        P(("dp", "ctx"), None),
        P(("dp", "ctx"), None),
        P(("dp", "ctx")),
        P(("dp", "ctx"), None),
        P("ctx", "dp", None),
        P("ctx", None, "dp"),
    )
    return jax.shard_map(
        on_device,
        mesh=mesh,
        in_specs=placed,
        out_specs=(
            P("dp", "ctx", None),
            P("dp", "ctx", None),
            P(("dp", "ctx")),
            P(("dp", "ctx"), None),
            P(("dp", "ctx"), None),
            P(("dp", "ctx"), None),
            P(("dp", "ctx"), None),
            P(("dp", "ctx")),
            P(("dp", "ctx"), None),
            P("ctx", "dp", None),
            P("ctx", None, "dp"),
        ),
        check_vma=False,
    )
```

profile of v0, /device:TPU:0, one launch (start us, length us, event | category | flops | bytes accessed | tf_op | source)
XLA Modules:
  0.0 2503.0 jit_solution(2861246156840205409)
XLA Ops:
  12.0 42.0 %all-reduce.14 = (bf16[1024]{0:T(1024)(128)(2,1)S(1)}, bf16[1024]{0:T(1024)(128)(2,1)S(1)}) all-reduce(bf16[1024]{0:T(1024)(128)(2,1)S(1)} %dynamic-update-slice, bf16[1024]{0:T(1024)(128)(2,1)S(1)} %dynamic-update-slice.1), channel_id=1, replica_groups=mesh['dp'=2,'ctx'=16] {'dp','ctx'}, use_global_device_ids=true, to_apply=%add.4 | all-reduce | flops 2048 | bytes 8192
  55.6 12.9 all-gather.23.cloned.1.call-done
  72.1 52.3 %all-gather.29.cloned.1.call-done = bf16[1024,512]{1,0:T(8,128)(2,1)} async-done(((bf16[32,512]{1,0:T(8,128)(2,1)}), bf16[1024,512]{1,0:T(8,128)(2,1)}) %all-gather.29.cloned.1.call-update) | async-done | bytes 1048592 | tf_op jit(solution)/shard_map/all_gather | solution.py:192
  128.8 9.0 reduce-window.16
  138.5 4.5 scatter_custom_fusion.1
  144.2 38.4 %all-gather.27.cloned.1.call-done = bf16[1024,1024]{1,0:T(8,128)(2,1)} async-done(((bf16[32,1024]{1,0:T(8,128)(2,1)}), bf16[1024,1024]{1,0:T(8,128)(2,1)}) %all-gather.27.cloned.1.call-update) | async-done | bytes 2097168 | tf_op jit(solution)/shard_map/all_gather | solution.py:190
  187.5 57.9 %all-gather.39.cloned.1.call-done = bf16[2048,512]{1,0:T(8,128)(2,1)} async-done(((bf16[128,512]{1,0:T(8,128)(2,1)}), bf16[2048,512]{1,0:T(8,128)(2,1)}) %all-gather.39.cloned.1.call-update) | async-done | bytes 2097168 | tf_op jit(solution)/shard_map/all_gather | solution.py:248
  249.5 58.4 %all-gather.41.cloned.1.call-done = bf16[2048,512]{1,0:T(8,128)(2,1)} async-done(((bf16[128,512]{1,0:T(8,128)(2,1)}), bf16[2048,512]{1,0:T(8,128)(2,1)}) %all-gather.41.cloned.1.call-update) | async-done | bytes 2097168 | tf_op jit(solution)/shard_map/all_gather | solution.py:249
  312.1 48.6 %while.61 = (s32[]{:T(128)}, f32[8,2,128]{2,1,0:T(2,128)S(1)}, f32[8,2,128]{2,1,0:T(2,128)S(1)}, f32[8,2,128,64]{2,3,1,0:T(8,128)S(1)}, s32[4]{0:T(128)S(1)}, /*...) while((s32[]{:T(128)}, f32[8,2,128]{2,1,0:T(2,128)S(1)}, ...), condition=%wide.region_18.19_spmd.clone, body=%wide.region_15.18_spmd.clone.sunk | while | flops 280570496 | bytes 34221800 | solution.py:87
  360.8 9.2 all-gather.25.cloned.1.call-done
  374.2 53.7 %all-gather.33.cloned.1.call-done = bf16[1024,1024]{1,0:T(8,128)(2,1)} async-done(((bf16[32,1024]{1,0:T(8,128)(2,1)}), bf16[1024,1024]{1,0:T(8,128)(2,1)}) %all-gather.33.cloned.1.call-update) | async-done | bytes 2097168 | tf_op jit(solution)/shard_map/all_gather | solution.py:193
  430.5 59.8 %all-gather.31.cloned.1.call-done = bf16[2048,512]{1,0:T(8,128)(2,1)} async-done(((bf16[128,512]{1,0:T(8,128)(2,1)}), bf16[2048,512]{1,0:T(8,128)(2,1)}) %all-gather.31.cloned.1.call-update) | async-done | bytes 2097168 | tf_op jit(solution)/shard_map/all_gather | solution.py:249
  494.5 48.3 %while.60 = (s32[]{:T(128)}, f32[8,2,128]{2,1,0:T(2,128)S(1)}, f32[8,2,128]{2,1,0:T(2,128)S(1)}, f32[8,2,128,64]{2,3,1,0:T(8,128)S(1)}, s32[4]{0:T(128)S(1)}, /*...) while((s32[]{:T(128)}, f32[8,2,128]{2,1,0:T(2,128)S(1)}, ...), condition=%wide.region_4.5_spmd.clone, body=%wide.region_1.4_spmd.clone.sunk | while | flops 280570496 | bytes 34221800 | solution.py:87
  545.9 5.2 gather_fusion.2
  551.1 4.5 all-to-all-start.2
  556.4 9.0 reduce-window.14
  570.6 5.1 gather_fusion
  575.6 31.9 %all-to-all-done.2 = bf16[16,2,40,1024]{3,2,1,0:T(8,128)(2,1)} async-done(((bf16[16,2,40,1024]{3,2,1,0:T(8,128)(2,1)}), bf16[16,2,40,1024]{3,2,1,0:T(8,128)(2,1)}, u32[]{:S(2)}, u32[]{:S(2)}) %all-to-all-start.2) | async-done | bytes 2621472 | tf_op jit(solution)/shard_map/all_to_all | solution.py:284
  607.6 12.0 all-to-all-start
  620.2 8.2 fusion.112
  628.4 5.0 all-gather.37.cloned.1.call-done
  633.4 4.8 convert_bitcast_fusion.2
  639.9 31.2 %all-to-all-done = bf16[16,2,40,1024]{3,2,1,0:T(8,128)(2,1)S(1)} async-done(((bf16[16,2,40,1024]{3,2,1,0:T(8,128)(2,1)}), bf16[16,2,40,1024]{3,2,1,0:T(8,128)(2,1)S(1)}, u32[]{:S(2)}, u32[]{:S(2)}) %all-to-all-start) | async-done | bytes 2621472 | tf_op jit(solution)/shard_map/all_to_all | solution.py:284
  672.6 12.0 all-to-all-start.3
  684.6 112.2 %all_gather.114 = bf16[1024,32]{1,0:T(8,128)(2,1)S(1)} all-gather(bf16[32,32]{1,0:T(8,128)(2,1)S(1)} %copy-done.73), channel_id=1, replica_groups=mesh['dp'=2,'ctx'=16] {'dp','ctx'}, dimensions={0}, use_global_device_ids=true | all-gather | bytes 67584 | tf_op jit(solution)/shard_map/all_gather | solution.py:195
  799.1 5.6 fusion.109
  813.2 5.3 gather_fusion.3
  824.0 5.1 gather_fusion.6
  829.1 35.6 %all-to-all-done.1 = bf16[16,2,40,1024]{3,2,1,0:T(8,128)(2,1)} async-done(((bf16[16,2,40,1024]{3,2,1,0:T(8,128)(2,1)}), bf16[16,2,40,1024]{3,2,1,0:T(8,128)(2,1)}, u32[]{:S(2)}, u32[]{:S(2)}) %all-to-all-start.1) | async-done | bytes 2621472 | tf_op jit(solution)/shard_map/all_to_all | solution.py:292
  864.7 12.2 all-to-all-start.6
  877.4 7.1 gather_fusion.1
  887.4 5.1 gather_fusion.4
  892.5 35.9 %all-to-all-done.6 = bf16[16,2,40,1024]{3,2,1,0:T(8,128)(2,1)} async-done(((bf16[16,2,40,1024]{3,2,1,0:T(8,128)(2,1)}), bf16[16,2,40,1024]{3,2,1,0:T(8,128)(2,1)}, u32[]{:S(2)}, u32[]{:S(2)}) %all-to-all-start.6) | async-done | bytes 2621472 | tf_op jit(solution)/shard_map/all_to_all | solution.py:317
  928.4 12.0 all-to-all-start.4
  941.1 8.2 fusion.106
  949.4 7.3 fusion.92
  961.7 30.1 %all-to-all-done.4 = bf16[16,2,40,1024]{3,2,1,0:T(8,128)(2,1)S(1)} async-done(((bf16[16,2,40,1024]{3,2,1,0:T(8,128)(2,1)}), bf16[16,2,40,1024]{3,2,1,0:T(8,128)(2,1)S(1)}, u32[]{:S(2)}, u32[]{:S(2)}) %all-to-all-start.4) | async-done | bytes 2621472 | tf_op jit(solution)/shard_map/all_to_all | solution.py:317
  993.3 12.0 all-to-all-start.7
  1005.9 8.3 fusion.103
  1014.2 6.4 fusion.96
  1025.7 34.2 %all-to-all-done.7 = bf16[16,2,40,1024]{3,2,1,0:T(8,128)(2,1)S(1)} async-done(((bf16[16,2,40,1024]{3,2,1,0:T(8,128)(2,1)}), bf16[16,2,40,1024]{3,2,1,0:T(8,128)(2,1)S(1)}, u32[]{:S(2)}, u32[]{:S(2)}) %all-to-all-start.7) | async-done | bytes 2621472 | tf_op jit(solution)/shard_map/all_to_all | solution.py:342
  1059.8 13.1 all-to-all-start.5
  1076.9 80.3 %all-reduce.13 = (bf16[1024]{0:T(1024)(128)(2,1)S(1)}, bf16[1024]{0:T(1024)(128)(2,1)}, bf16[1024]{0:T(1024)(128)(2,1)S(1)}, bf16[1024]{0:T(1024)(128)(2,1)}) all-reduce(bf16[1024]{0:T(1024)(128)(2,1)S(1)} %dynamic-update-slice.4, bf16[1024]{0:T(1024)(128)(2,1)S(1)} %dynamic-update-slice.5, ...), channel_id=1, replica_groups=mesh['dp'=2,'ctx'=16] {'dp','ctx'}, use_global_device_ids=true, to_apply=%add.8 | all-reduce | flops 4096 | bytes 16384
  1157.2 72.4 %all_gather.128 = bf16[1024,32]{1,0:T(8,128)(2,1)} all-gather(bf16[32,32]{1,0:T(8,128)(2,1)S(1)} %copy-done.73), channel_id=1, replica_groups=mesh['dp'=2,'ctx'=16] {'dp','ctx'}, dimensions={0}, use_global_device_ids=true | all-gather | bytes 67584 | tf_op jit(solution)/shard_map/all_gather | solution.py:195
  1229.6 65.1 %all_gather.119 = bf16[1024,32]{1,0:T(8,128)(2,1)S(1)} all-gather(bf16[32,32]{1,0:T(8,128)(2,1)S(1)} %copy-done.73), channel_id=1, replica_groups=mesh['dp'=2,'ctx'=16] {'dp','ctx'}, dimensions={0}, use_global_device_ids=true | all-gather | bytes 67584 | tf_op jit(solution)/shard_map/all_gather | solution.py:195
  1294.8 5.4 gather_fusion.7
  1300.2 8.2 gather_fusion.5
  1323.7 88.1 %while.62 = (s32[]{:T(128)}, f32[8,2,128,64]{2,3,1,0:T(8,128)}, bf16[4,512,512]{2,1,0:T(8,128)(2,1)}, bf16[4,512,512]{2,1,0:T(8,128)(2,1)}, s32[4]{0:T(128)S(1)}...) while((s32[]{:T(128)}, f32[8,2,128,64]{2,3,1,0:T(8,128)}, ...), condition=%wide.region_35.36_spmd.clone, body=%wide.region_34.35_spmd.clone.sunk | while | flops 682689152 | bytes 48992572 | solution.py:141
  1415.1 88.4 %while.63 = (s32[]{:T(128)}, f32[8,2,128,64]{2,3,1,0:T(8,128)}, bf16[4,512,512]{2,1,0:T(8,128)(2,1)}, bf16[4,512,512]{2,1,0:T(8,128)(2,1)}, s32[4]{0:T(128)S(1)}...) while((s32[]{:T(128)}, f32[8,2,128,64]{2,3,1,0:T(8,128)}, ...), condition=%wide.region_46.47_spmd.clone, body=%wide.region_45.46_spmd.clone.sunk | while | flops 682689152 | bytes 47943976 | solution.py:141
  1504.8 5.4 fusion.115
  1510.2 6.0 fusion.73
  1517.8 5.4 fusion.99
  1523.3 6.9 fusion.68
  1542.1 44.4 %reduce-scatter.18.cloned.1.call-done = bf16[128,512]{1,0:T(8,128)(2,1)} async-done(((bf16[2048,512]{1,0:T(8,128)(2,1)}), bf16[128,512]{1,0:T(8,128)(2,1)}) %reduce-scatter.18.cloned.1.call-update) | async-done | bytes 131088 | tf_op jit(solution)/shard_map/reduce_scatter | solution.py:385
  1590.3 79.5 %reduce-scatter.16.cloned.1.call-done = bf16[128,512]{1,0:T(8,128)(2,1)} async-done(((bf16[2048,512]{1,0:T(8,128)(2,1)}), bf16[128,512]{1,0:T(8,128)(2,1)}) %reduce-scatter.16.cloned.1.call-update) | async-done | bytes 131088 | tf_op jit(solution)/shard_map/reduce_scatter | solution.py:382
  1670.9 80.1 %reduce-scatter.12.cloned.1.call-done = bf16[128,512]{1,0:T(8,128)(2,1)} async-done(((bf16[2048,512]{1,0:T(8,128)(2,1)}), bf16[128,512]{1,0:T(8,128)(2,1)}) %reduce-scatter.12.cloned.1.call-update) | async-done | bytes 131088 | tf_op jit(solution)/shard_map/reduce_scatter | solution.py:382
  1771.3 4.6 reduce-scatter.30.cloned.1.call-done
  1783.5 32.9 %all-gather.53.cloned.1.call-done = bf16[1024,512]{1,0:T(8,128)(2,1)} async-done(((bf16[32,512]{1,0:T(8,128)(2,1)}), bf16[1024,512]{1,0:T(8,128)(2,1)}) %all-gather.53.cloned.1.call-update) | async-done | bytes 1048592 | tf_op jit(solution)/shard_map/all_gather | solution.py:192
  1818.2 54.6 %all-gather.65.cloned.1.call-done = bf16[1024,512]{1,0:T(8,128)(2,1)} async-done(((bf16[32,512]{1,0:T(8,128)(2,1)}), bf16[1024,512]{1,0:T(8,128)(2,1)}) %all-gather.65.cloned.1.call-update) | async-done | bytes 1048592 | tf_op jit(solution)/shard_map/all_gather | solution.py:192
  1874.6 39.5 %all-reduce.12 = (f32[1024]{0:T(1024)S(1)}, f32[1024]{0:T(1024)S(1)}) all-reduce(f32[1024]{0:T(1024)S(1)} %add.411, f32[1024]{0:T(1024)S(1)} %add.418), channel_id=6, replica_groups=mesh['dp'=2,'ctx'=16] {'dp','ctx'}, use_global_device_ids=true, to_apply=%region_52.53.clone | all-reduce | flops 2048 | bytes 16384
  1917.2 145.6 %reduce-scatter.26.cloned.1.call-done = f32[32,1024]{1,0:T(8,128)} async-done(((f32[1024,1024]{1,0:T(8,128)}), f32[32,1024]{1,0:T(8,128)}) %reduce-scatter.26.cloned.1.call-update) | async-done | bytes 131088 | tf_op jit(solution)/shard_map/reduce_scatter | solution.py:424
  2062.8 144.6 %reduce-scatter.24.cloned.1.call-done = f32[32,512]{1,0:T(8,128)} async-done(((f32[1024,512]{1,0:T(8,128)}), f32[32,512]{1,0:T(8,128)}) %reduce-scatter.24.cloned.1.call-update) | async-done | bytes 65552 | tf_op jit(solution)/shard_map/reduce_scatter | solution.py:423
  2207.3 141.8 %reduce-scatter.22.cloned.1.call-done = f32[32,512]{1,0:T(8,128)} async-done(((f32[1024,512]{1,0:T(8,128)}), f32[32,512]{1,0:T(8,128)}) %reduce-scatter.22.cloned.1.call-update) | async-done | bytes 65552 | tf_op jit(solution)/shard_map/reduce_scatter | solution.py:422
  2349.1 146.2 %reduce-scatter.20.cloned.1.call-done = f32[32,1024]{1,0:T(8,128)} async-done(((f32[1024,1024]{1,0:T(8,128)}), f32[32,1024]{1,0:T(8,128)}) %reduce-scatter.20.cloned.1.call-update) | async-done | bytes 131088 | tf_op jit(solution)/shard_map/reduce_scatter | solution.py:421
  (758 shorter events, 401.4 us)
Async XLA Ops:
  8.0 62.0 %copy-start.8 = (bf16[2,128,1024]{2,1,0:T(8,128)(2,1)S(1)}, bf16[2,128,1024]{2,1,0:T(8,128)(2,1)}, u32[]{:S(2)}) copy-start(bf16[2,128,1024]{2,1,0:T(8,128)(2,1)} %param.21) | copy-start | bytes 1572868
  8.0 60.5 %all-gather.23.cloned.1.call-start = ((), (), s32[]{:S(2)}) async-start(), calls=%async_computation.19 | async-start | bytes 1081344 | tf_op jit(solution)/shard_map/all_gather | solution.py:191
  8.8 115.6 %all-gather.29.cloned.1.call-start = ((), (), s32[]{:S(2)}) async-start(), calls=%async_computation.22 | async-start | bytes 1081344 | tf_op jit(solution)/shard_map/all_gather | solution.py:192
  9.5 173.1 %all-gather.27.cloned.1.call-start = ((), (), s32[]{:S(2)}) async-start(), calls=%async_computation.21 | async-start | bytes 2162688 | tf_op jit(solution)/shard_map/all_gather | solution.py:190
  10.2 235.1 %all-gather.39.cloned.1.call-start = ((), (), s32[]{:S(2)}) async-start(), calls=%async_computation.27 | async-start | bytes 2228224 | tf_op jit(solution)/shard_map/all_gather | solution.py:248
  54.0 132.2 %copy-start.59 = (f32[1024]{0:T(1024)}, f32[1024]{0:T(1024)S(1)}, u32[]{:S(2)}) copy-start(f32[1024]{0:T(1024)S(1)} %convert_element_type.342) | copy-start | bytes 12292
  54.2 133.0 %copy-start.44 = (f32[128,64]{0,1:T(8,128)}, f32[128,64]{0,1:T(8,128)S(1)}, u32[]{:S(2)}) copy-start(f32[128,64]{0,1:T(8,128)S(1)} %get-tuple-element.962) | copy-start | bytes 98308
  54.2 133.0 %copy-start.52 = (f32[128,64]{0,1:T(8,128)}, f32[128,64]{0,1:T(8,128)S(1)}, u32[]{:S(2)}) copy-start(f32[128,64]{0,1:T(8,128)S(1)} %get-tuple-element.963) | copy-start | bytes 98308
  55.6 129.9 %copy-start.78 = (f32[128]{0:T(128)}, f32[128]{0:T(128)S(1)}, u32[]{:S(2)}) copy-start(f32[128]{0:T(128)S(1)} %add_rsqrt_fusion.1) | copy-start | bytes 1540
  55.6 130.7 %copy-start.80 = (f32[128]{0:T(128)}, f32[128]{0:T(128)S(1)}, u32[]{:S(2)}) copy-start(f32[128]{0:T(128)S(1)} %add_rsqrt_fusion.3) | copy-start | bytes 1540
  71.1 57.4 %copy-start.85 = (s32[2,128,8]{1,2,0:T(8,128)S(1)}, s32[2,128,8]{1,2,0:T(8,128)}, u32[]{:S(2)}) copy-start(s32[2,128,8]{1,2,0:T(8,128)} %param.23) | copy-start | bytes 24580
  71.1 71.9 %copy-start.84 = (s32[2,2048]{1,0:T(2,128)S(1)}, s32[2,2048]{1,0:T(2,128)}, u32[]{:S(2)}) copy-start(s32[2,2048]{1,0:T(2,128)} %param.22) | copy-start | bytes 49156
  72.0 235.9 %all-gather.41.cloned.1.call-start = ((), (), s32[]{:S(2)}) async-start(), calls=%async_computation.28 | async-start | bytes 2228224 | tf_op jit(solution)/shard_map/all_gather | solution.py:249
  126.7 243.3 %all-gather.25.cloned.1.call-start = ((), (), s32[]{:S(2)}) async-start(), calls=%async_computation.20 | async-start | bytes 2228224 | tf_op jit(solution)/shard_map/all_gather | solution.py:248
  127.6 300.4 %all-gather.33.cloned.1.call-start = ((), (), s32[]{:S(2)}) async-start(), calls=%async_computation.24 | async-start | bytes 2162688 | tf_op jit(solution)/shard_map/all_gather | solution.py:193
  128.3 362.0 %all-gather.31.cloned.1.call-start = ((), (), s32[]{:S(2)}) async-start(), calls=%async_computation.23 | async-start | bytes 2228224 | tf_op jit(solution)/shard_map/all_gather | solution.py:249
  249.5 62.6 %copy-start.57 = (f32[8,2,128,64]{2,3,1,0:T(8,128)S(1)}, f32[8,2,128,64]{2,3,1,0:T(8,128)}, u32[]{:S(2)}) copy-start(f32[8,2,128,64]{2,3,1,0:T(8,128)} %custom-call.5) | copy-start | bytes 1572868
  374.2 120.2 %copy-start.18 = (f32[8,2,128,64]{2,3,1,0:T(8,128)}, f32[8,2,128,64]{2,3,1,0:T(8,128)S(1)}, u32[]{:S(2)}) copy-start(f32[8,2,128,64]{2,3,1,0:T(8,128)S(1)} %broadcast_divide_fusion) | copy-start | bytes 1572868
  430.4 115.2 %copy-start.23 = (f32[128,1024]{1,0:T(8,128)}, f32[128,1024]{1,0:T(8,128)S(1)}, u32[]{:S(2)}) copy-start(f32[128,1024]{1,0:T(8,128)S(1)} %get-tuple-element.954) | copy-start | bytes 1572868
  430.4 64.0 %copy-start.56 = (f32[8,2,128,64]{2,3,1,0:T(8,128)S(1)}, f32[8,2,128,64]{2,3,1,0:T(8,128)}, u32[]{:S(2)}) copy-start(f32[8,2,128,64]{2,3,1,0:T(8,128)} %custom-call.2) | copy-start | bytes 1572868
  430.5 115.2 %copy-start.86 = (f32[128]{0:T(128)}, f32[128]{0:T(128)S(1)}, u32[]{:S(2)}) copy-start(f32[128]{0:T(128)S(1)} %add_rsqrt_fusion) | copy-start | bytes 1540
  545.8 253.0 %copy-start.28 = (bf16[128,1024]{1,0:T(8,128)(2,1)}, bf16[128,1024]{1,0:T(8,128)(2,1)S(1)}, u32[]{:S(2)}) copy-start(bf16[128,1024]{1,0:T(8,128)(2,1)S(1)} %get-tuple-element.948) | copy-start | bytes 786436
  551.1 56.5 %all-to-all-start.2 = ((bf16[16,2,40,1024]{3,2,1,0:T(8,128)(2,1)}), bf16[16,2,40,1024]{3,2,1,0:T(8,128)(2,1)}, u32[]{:S(2)}, u32[]{:S(2)}) async-start(bf16[16,2,40,1024]{3,2,1,0:T(8,128)(2,1)} %bitcast.46), calls=%async_computation.2 | async-start | bytes 5242880 | tf_op jit(solution)/shard_map/all_to_all | solution.py:284
  555.5 64.7 %all-gather.35.cloned.1.call-start = ((), (), s32[]{:S(2)}) async-start(), calls=%async_computation.25 | async-start | bytes 6291456 | tf_op jit(solution)/shard_map/all_gather | solution.py:200
  607.6 63.5 %all-to-all-start = ((bf16[16,2,40,1024]{3,2,1,0:T(8,128)(2,1)}), bf16[16,2,40,1024]{3,2,1,0:T(8,128)(2,1)S(1)}, u32[]{:S(2)}, u32[]{:S(2)}) async-start(bf16[16,2,40,1024]{3,2,1,0:T(8,128)(2,1)} %bitcast.20), calls=%async_computation | async-start | bytes 5242880 | tf_op jit(solution)/shard_map/all_to_all | solution.py:284
  619.6 13.8 all-gather.37.cloned.1.call-start
  672.6 135.6 %all-to-all-start.3 = ((bf16[16,2,40,1024]{3,2,1,0:T(8,128)(2,1)}), bf16[16,2,40,1024]{3,2,1,0:T(8,128)(2,1)S(1)}, u32[]{:S(2)}, u32[]{:S(2)}) async-start(bf16[16,2,40,1024]{3,2,1,0:T(8,128)(2,1)} %copy.263), calls=%async_computation.3 | async-start | bytes 5242880 | tf_op jit(solution)/shard_map/all_to_all | solution.py:292
  808.2 56.5 %all-to-all-start.1 = ((bf16[16,2,40,1024]{3,2,1,0:T(8,128)(2,1)}), bf16[16,2,40,1024]{3,2,1,0:T(8,128)(2,1)}, u32[]{:S(2)}, u32[]{:S(2)}) async-start(bf16[16,2,40,1024]{3,2,1,0:T(8,128)(2,1)} %copy.252), calls=%async_computation.1 | async-start | bytes 5242880 | tf_op jit(solution)/shard_map/all_to_all | solution.py:292
  812.7 128.5 %all-gather.55.cloned.1.call-start = ((), (), s32[]{:S(2)}) async-start(), calls=%async_computation.37 | async-start | bytes 6291456 | tf_op jit(solution)/shard_map/all_gather | solution.py:200
  822.8 126.6 %all-gather.57.cloned.1.call-start = ((), (), s32[]{:S(2)}) async-start(), calls=%async_computation.38 | async-start | bytes 3145728 | tf_op jit(solution)/shard_map/all_gather | solution.py:201
  864.7 63.7 %all-to-all-start.6 = ((bf16[16,2,40,1024]{3,2,1,0:T(8,128)(2,1)}), bf16[16,2,40,1024]{3,2,1,0:T(8,128)(2,1)}, u32[]{:S(2)}, u32[]{:S(2)}) async-start(bf16[16,2,40,1024]{3,2,1,0:T(8,128)(2,1)} %bitcast.700), calls=%async_computation.8 | async-start | bytes 5242880 | tf_op jit(solution)/shard_map/all_to_all | solution.py:317
  876.9 129.0 %all-gather.43.cloned.1.call-start = ((), (), s32[]{:S(2)}) async-start(), calls=%async_computation.29 | async-start | bytes 6291456 | tf_op jit(solution)/shard_map/all_gather | solution.py:200
  928.4 63.4 %all-to-all-start.4 = ((bf16[16,2,40,1024]{3,2,1,0:T(8,128)(2,1)}), bf16[16,2,40,1024]{3,2,1,0:T(8,128)(2,1)S(1)}, u32[]{:S(2)}, u32[]{:S(2)}) async-start(bf16[16,2,40,1024]{3,2,1,0:T(8,128)(2,1)} %bitcast.701), calls=%async_computation.4 | async-start | bytes 5242880 | tf_op jit(solution)/shard_map/all_to_all | solution.py:317
  940.4 73.8 %all-gather.45.cloned.1.call-start = ((), (), s32[]{:S(2)}) async-start(), calls=%async_computation.30 | async-start | bytes 3145728 | tf_op jit(solution)/shard_map/all_gather | solution.py:201
  993.3 66.5 %all-to-all-start.7 = ((bf16[16,2,40,1024]{3,2,1,0:T(8,128)(2,1)}), bf16[16,2,40,1024]{3,2,1,0:T(8,128)(2,1)S(1)}, u32[]{:S(2)}, u32[]{:S(2)}) async-start(bf16[16,2,40,1024]{3,2,1,0:T(8,128)(2,1)} %copy.285), calls=%async_computation.9 | async-start | bytes 5242880 | tf_op jit(solution)/shard_map/all_to_all | solution.py:342
  1005.3 309.3 %all-gather.59.cloned.1.call-start = ((), (), s32[]{:S(2)}) async-start(), calls=%async_computation.39 | async-start | bytes 2162688 | tf_op jit(solution)/shard_map/all_gather | solution.py:193
  1025.6 50.2 %copy-start.51 = (f32[8,2,128]{2,1,0:T(2,128)S(1)}, f32[8,2,128]{2,1,0:T(2,128)}, u32[]{:S(2)}) copy-start(f32[8,2,128]{2,1,0:T(2,128)} %copy-done.50) | copy-start | bytes 24580
  1025.6 50.2 %copy-start.62 = (f32[8,2,128]{2,1,0:T(2,128)S(1)}, f32[8,2,128]{2,1,0:T(2,128)}, u32[]{:S(2)}) copy-start(f32[8,2,128]{2,1,0:T(2,128)} %copy-done.61) | copy-start | bytes 24580
  1025.6 50.4 %copy-start.96 = (bf16[32]{0:T(256)(128)(2,1)S(1)}, bf16[32]{0:T(256)(128)(2,1)}, u32[]{:S(2)}) copy-start(bf16[32]{0:T(256)(128)(2,1)} %param.25) | copy-start | bytes 196
  1025.6 50.6 %copy-start.97 = (bf16[32]{0:T(256)(128)(2,1)S(1)}, bf16[32]{0:T(256)(128)(2,1)}, u32[]{:S(2)}) copy-start(bf16[32]{0:T(256)(128)(2,1)} %param.30) | copy-start | bytes 196
  1059.8 240.4 %all-to-all-start.5 = ((bf16[16,2,40,1024]{3,2,1,0:T(8,128)(2,1)}), bf16[16,2,40,1024]{3,2,1,0:T(8,128)(2,1)}, u32[]{:S(2)}, u32[]{:S(2)}) async-start(bf16[16,2,40,1024]{3,2,1,0:T(8,128)(2,1)} %copy.269), calls=%async_computation.5 | async-start | bytes 5242880 | tf_op jit(solution)/shard_map/all_to_all | solution.py:342
  1072.9 245.2 %all-gather.47.cloned.1.call-start = ((), (), s32[]{:S(2)}) async-start(), calls=%async_computation.31 | async-start | bytes 2162688 | tf_op jit(solution)/shard_map/all_gather | solution.py:193
  1073.5 464.8 %reduce-scatter.14.cloned.1.call-start = ((), (), s32[]{:S(2)}) async-start(), calls=%async_computation.35 | async-start | bytes 2228224 | tf_op jit(solution)/shard_map/reduce_scatter | solution.py:385
  1411.8 174.6 %reduce-scatter.18.cloned.1.call-start = ((), (), s32[]{:S(2)}) async-start(), calls=%async_computation.43 | async-start | bytes 2228224 | tf_op jit(solution)/shard_map/reduce_scatter | solution.py:385
  1503.5 166.3 %reduce-scatter.16.cloned.1.call-start = ((), (), s32[]{:S(2)}) async-start(), calls=%async_computation.41 | async-start | bytes 2228224 | tf_op jit(solution)/shard_map/reduce_scatter | solution.py:382
  1504.2 246.7 %reduce-scatter.12.cloned.1.call-start = ((), (), s32[]{:S(2)}) async-start(), calls=%async_computation.33 | async-start | bytes 2228224 | tf_op jit(solution)/shard_map/reduce_scatter | solution.py:382
  1504.8 256.0 %reduce-scatter.32.cloned.1.call-start = ((), (), s32[]{:S(2)}) async-start(), calls=%async_computation.51 | async-start | bytes 3145728 | tf_op jit(solution)/shard_map/reduce_scatter | solution.py:432
  1516.2 249.3 %all-gather.61.cloned.1.call-start = ((), (), s32[]{:S(2)}) async-start(), calls=%async_computation.40 | async-start | bytes 2162688 | tf_op jit(solution)/shard_map/all_gather | solution.py:190
  1516.8 251.2 %all-gather.49.cloned.1.call-start = ((), (), s32[]{:S(2)}) async-start(), calls=%async_computation.32 | async-start | bytes 2162688 | tf_op jit(solution)/shard_map/all_gather | solution.py:190
  1517.5 258.3 %reduce-scatter.30.cloned.1.call-start = ((), (), s32[]{:S(2)}) async-start(), calls=%async_computation.50 | async-start | bytes 6291456 | tf_op jit(solution)/shard_map/reduce_scatter | solution.py:429
  1530.3 249.6 %all-gather.63.cloned.1.call-start = ((), (), s32[]{:S(2)}) async-start(), calls=%async_computation.42 | async-start | bytes 1081344 | tf_op jit(solution)/shard_map/all_gather | solution.py:191
  1530.9 250.8 %all-gather.51.cloned.1.call-start = ((), (), s32[]{:S(2)}) async-start(), calls=%async_computation.34 | async-start | bytes 1081344 | tf_op jit(solution)/shard_map/all_gather | solution.py:191
  1531.6 284.8 %all-gather.53.cloned.1.call-start = ((), (), s32[]{:S(2)}) async-start(), calls=%async_computation.36 | async-start | bytes 1081344 | tf_op jit(solution)/shard_map/all_gather | solution.py:192
  1532.2 340.6 %all-gather.65.cloned.1.call-start = ((), (), s32[]{:S(2)}) async-start(), calls=%async_computation.44 | async-start | bytes 1081344 | tf_op jit(solution)/shard_map/all_gather | solution.py:192
  1532.9 384.2 %reduce-scatter.28.cloned.1.call-start = ((), (), s32[]{:S(2)}) async-start(), calls=%async_computation.49 | async-start | bytes 540672 | tf_op jit(solution)/shard_map/reduce_scatter | solution.py:426
  1534.4 528.4 %reduce-scatter.26.cloned.1.call-start = ((), (), s32[]{:S(2)}) async-start(), calls=%async_computation.48 | async-start | bytes 4325376 | tf_op jit(solution)/shard_map/reduce_scatter | solution.py:424
  1538.3 48.2 %copy-start.79 = (f32[128]{0:T(128)S(1)}, f32[128]{0:T(128)}, u32[]{:S(2)}) copy-start(f32[128]{0:T(128)} %copy-done.78) | copy-start | bytes 1540
  1538.3 669.1 %reduce-scatter.24.cloned.1.call-start = ((), (), s32[]{:S(2)}) async-start(), calls=%async_computation.47 | async-start | bytes 2162688 | tf_op jit(solution)/shard_map/reduce_scatter | solution.py:423
  1542.1 48.0 %copy-start.45 = (f32[128,64]{0,1:T(8,128)S(1)}, f32[128,64]{0,1:T(8,128)}, u32[]{:S(2)}) copy-start(f32[128,64]{0,1:T(8,128)} %copy-done.44) | copy-start | bytes 98308
  1590.0 162.0 %copy-start.53 = (f32[128,64]{0,1:T(8,128)S(1)}, f32[128,64]{0,1:T(8,128)}, u32[]{:S(2)}) copy-start(f32[128,64]{0,1:T(8,128)} %copy-done.52) | copy-start | bytes 98308
  1590.1 759.0 %reduce-scatter.22.cloned.1.call-start = ((), (), s32[]{:S(2)}) async-start(), calls=%async_computation.46 | async-start | bytes 2162688 | tf_op jit(solution)/shard_map/reduce_scatter | solution.py:422
  1669.8 82.7 %copy-start.54 = (bf16[128,512]{1,0:T(8,128)(2,1)S(1)}, bf16[128,512]{1,0:T(8,128)(2,1)}, u32[]{:S(2)}) copy-start(bf16[128,512]{1,0:T(8,128)(2,1)} %reduce-scatter.16.cloned.1.call-done) | copy-start | bytes 393220
  1755.0 740.3 %reduce-scatter.20.cloned.1.call-start = ((), (), s32[]{:S(2)}) async-start(), calls=%async_computation.45 | async-start | bytes 4325376 | tf_op jit(solution)/shard_map/reduce_scatter | solution.py:421
  1781.6 91.1 %copy-start.58 = (bf16[128,512]{1,0:T(8,128)(2,1)S(1)}, bf16[128,512]{1,0:T(8,128)(2,1)}, u32[]{:S(2)}) copy-start(bf16[128,512]{1,0:T(8,128)(2,1)} %reduce-scatter.18.cloned.1.call-done) | copy-start | bytes 393220
  (104 other events, 568.2 us)
Sparse Core Ops, SparseCore 0:
  11.9 56.5 all-gather.22
  71.6 52.7 all-gather.28
  127.2 55.3 all-gather.26
  185.8 59.5 all-gather.38
  248.6 59.3 all-gather.40
  310.6 59.3 all-gather.24
  372.8 55.0 all-gather.32
  430.7 59.5 all-gather.30
  1411.9 80.9 reduce-scatter.13
  1503.6 82.8 reduce-scatter.17
  1588.7 81.0 reduce-scatter.15
  1671.9 78.9 reduce-scatter.11
  1753.2 6.5 reduce-scatter.31
  1762.6 13.1 reduce-scatter.29
  1778.5 138.6 reduce-scatter.27
  1920.0 142.7 reduce-scatter.25
  2065.5 141.7 reduce-scatter.23
  2210.0 139.0 reduce-scatter.21
  2352.0 143.2 reduce-scatter.19
Sparse Core Ops, SparseCore 1:
  557.6 14.7 all-gather.34
  621.6 11.7 all-gather.36
  822.9 14.7 all-gather.54
  839.2 11.6 all-gather.56
  886.9 14.8 all-gather.42
  942.7 11.7 all-gather.44
  1008.6 86.1 all-gather.58
  1097.5 65.6 all-gather.46
  1519.6 60.9 all-gather.60
  1583.4 62.0 all-gather.48
  1648.5 55.0 all-gather.62
  1706.6 53.1 all-gather.50
  1762.7 53.6 all-gather.52
  1819.5 53.2 all-gather.64
where the time goes:
time: 2510 us; the launch traced here: 2500 us
  waiting for transfers between devices  1430 us (57%)
  blocking collectives  411 us (16%)
  matrix products  238 us (9%)
  local copies, waits for them, and re-layouts  201 us (8%)
  other arithmetic  85.4 us (3%)
  starting transfers between devices  85.2 us (3%)
  loops' own time  32.2 us (1%)
    all_gather x3, blocking collectives, gather_layer(): lax.all_gather(shards[6], ('dp', 'ctx'), axis=0, tiled=True)  250 us
    unnamed x3, blocking collectives  162 us
    reduce_scatter x2, waiting for transfers between devices, on_device(): lax.psum_scatter(grad_keys.astype(jnp.bfloat16), 'ctx', scatter_dimension...  160 us
    reduce_scatter x1, waiting for transfers between devices, on_device(): lax.psum_scatter(acc_query, ('dp', 'ctx'), scatter_dimension=0, tiled=True)  146 us
    reduce_scatter x1, waiting for transfers between devices, on_device(): lax.psum_scatter(acc_proj, ('dp', 'ctx'), scatter_dimension=0, tiled=True)  146 us
    reduce_scatter x1, waiting for transfers between devices, on_device(): lax.psum_scatter(acc_value, ('dp', 'ctx'), scatter_dimension=0, tiled=True)  145 us
    reduce_scatter x1, waiting for transfers between devices, on_device(): lax.psum_scatter(acc_key, ('dp', 'ctx'), scatter_dimension=0, tiled=True)  142 us
    all_gather x3, waiting for transfers between devices, gather_layer(): lax.all_gather(shards[3], ('dp', 'ctx'), axis=0, tiled=True)  140 us
  transfers between devices with their start and end apart: 41, of which 26 were waited for; matrix products, arithmetic and copies ran while one was open for 15% of the time, Pallas kernels for 0%

commit v1 on v0

v1 whole, which is shorter than its diff:
```python
import math

import jax
import jax.numpy as jnp
from jax import lax
from jax.sharding import PartitionSpec as P

HEADS = 16
KV_HEADS = 8
HEAD_DIM = 64


EPS = 1e-06
ROPE_BASE = 10000.0
NEG = -1e30


def rope_tables(positions, head_dim):
    steps_f = jnp.arange(0, head_dim, 2, dtype=jnp.float32)
    inv_freq = jnp.exp(-math.log(ROPE_BASE) * steps_f / head_dim)
    angle = positions.astype(jnp.float32)[:, None] * inv_freq[None, :]
    cosine = jnp.concatenate([jnp.cos(angle), jnp.cos(angle)], -1)[:, None, :]
    sine_table = jnp.concatenate([jnp.sin(angle), jnp.sin(angle)], -1)[:, None, :]
    return (cosine, sine_table)


def rotate(tensor, cosine, sine_table):
    half = tensor.shape[-1] // 2
    turned = jnp.concatenate([-tensor[..., half:], tensor[..., :half]], -1)
    return tensor * cosine + turned * sine_table


def rotate_back(gradient, cosine, sine_table):
    half = gradient.shape[-1] // 2
    scaled = gradient * sine_table
    turned = jnp.concatenate([scaled[..., half:], -scaled[..., :half]], -1)
    return gradient * cosine + turned


def norm_back(gradient, normed, inverse, gain_vec):
    scaled = gradient * gain_vec
    return inverse * (scaled - normed * jnp.mean(scaled * normed, -1, keepdims=True))


def split_blocks(pieces):
    amount = pieces[0].shape[0]
    block_size = math.gcd(amount, 512)
    number = amount // block_size
    split_parts = tuple((piece.reshape((number, block_size) + piece.shape[1:]) for piece in pieces))
    starts = jnp.arange(number, dtype=jnp.int32) * block_size
    return (split_parts, starts, block_size)


def block_mask(key_start, block_size, query_pos, query_seg, seg_row):
    key_pos = key_start + jnp.arange(block_size, dtype=jnp.int32)
    key_seg = lax.dynamic_slice_in_dim(seg_row, key_start, block_size)
    return (key_pos[None, :] <= query_pos[:, None]) & (key_seg[None, :] == query_seg[:, None])


def attend_forward(carried, pieces, queries, query_pos, query_seg, seg_row, score_scale):
    kv_heads = queries.shape[1]
    head_dim = queries.shape[3]
    split_parts, starts, block_size = split_blocks(pieces)

    def one_block(run_state, block_inputs):
        run_max, run_sum, run_acc = run_state
        key_block, value_block, key_start = block_inputs
        key_heads = key_block.reshape(block_size, kv_heads, head_dim)
        value_heads = value_block.reshape(block_size, kv_heads, head_dim)
        allowed = block_mask(key_start, block_size, query_pos, query_seg, seg_row)
        scores = (
            jnp.einsum("qhgd,khd->hgqk", queries, key_heads, preferred_element_type=jnp.float32)
            * score_scale
        )
        new_max = jnp.maximum(run_max, jnp.max(jnp.where(allowed, scores, NEG), -1))
        factor = jnp.exp(run_max - new_max)
        weights_exp = jnp.where(allowed, jnp.exp(scores - new_max[..., None]), 0.0)
        run_sum = run_sum * factor + jnp.sum(weights_exp, -1)
        run_acc = run_acc * factor[..., None] + jnp.einsum(
            "hgqk,khd->hgqd",
            weights_exp.astype(jnp.bfloat16),
            value_heads,
            preferred_element_type=jnp.float32,
        )
        return ((new_max, run_sum, run_acc), None)

    final_state, unused = lax.scan(one_block, carried, (split_parts[0], split_parts[1], starts))
    return final_state


def attend_backward(
    carried,
    pieces,
    queries,
    query_pos,
    query_seg,
    seg_row,
    score_scale,
    grad_heads,
    log_sum,
    delta_rows,
):
    grad_query, grad_keys, grad_values = carried
    kv_heads = queries.shape[1]
    head_dim = queries.shape[3]
    split_parts, starts, block_size = split_blocks(pieces)

    def one_block(grad_acc, block_inputs):
        key_block, value_block, key_start = block_inputs
        key_heads = key_block.reshape(block_size, kv_heads, head_dim)
        value_heads = value_block.reshape(block_size, kv_heads, head_dim)
        allowed = block_mask(key_start, block_size, query_pos, query_seg, seg_row)
        scores = (
            jnp.einsum("qhgd,khd->hgqk", queries, key_heads, preferred_element_type=jnp.float32)
            * score_scale
        )
        probs_full = jnp.where(allowed, jnp.exp(scores - log_sum[..., None]), 0.0)
        grad_value = jnp.einsum(
            "hgqk,qhgd->khd",
            probs_full.astype(jnp.bfloat16),
            grad_heads,
            preferred_element_type=jnp.float32,
        )
        grad_prob = jnp.einsum(
            "qhgd,khd->hgqk", grad_heads, value_heads, preferred_element_type=jnp.float32
        )
        grad_score = (probs_full * (grad_prob - delta_rows[..., None])).astype(jnp.bfloat16)
        grad_acc = (
            grad_acc
            + jnp.einsum(
                "hgqk,khd->hgqd", grad_score, key_heads, preferred_element_type=jnp.float32
            )
            * score_scale
        )
        grad_key = (
            jnp.einsum("hgqk,qhgd->khd", grad_score, queries, preferred_element_type=jnp.float32)
            * score_scale
        )
        return (grad_acc, (grad_key.reshape(block_size, -1), grad_value.reshape(block_size, -1)))

    grad_query, (key_parts, value_parts) = lax.scan(
        one_block, grad_query, (split_parts[0], split_parts[1], starts)
    )
    kv_width = grad_keys.shape[1]
    grad_keys = key_parts.reshape(-1, kv_width)
    grad_values = value_parts.reshape(-1, kv_width)
    return (grad_query, grad_keys, grad_values)


def attention_forward(queries, keys_all, values_all, query_pos, query_segs, segments, score_scale):
    micro, span_len, kv_heads, groups, head_dim = queries.shape
    f32 = jnp.float32
    start_state = (
        jnp.full((kv_heads, groups, span_len), NEG, f32),
        jnp.zeros((kv_heads, groups, span_len), f32),
        jnp.zeros((kv_heads, groups, span_len, head_dim), f32),
    )

    def one(query_rows, key_rows, value_rows, query_seg, seg_row):
        return attend_forward(
            start_state,
            (key_rows, value_rows),
            query_rows,
            query_pos,
            query_seg,
            seg_row,
            score_scale,
        )

    run_max, run_sum, run_acc = jax.vmap(one)(
        queries, keys_all, values_all, query_segs, segments
    )
    return run_acc / run_sum[..., None], run_max + jnp.log(run_sum)


def attention_backward(
    queries,
    keys_all,
    values_all,
    query_pos,
    query_segs,
    segments,
    score_scale,
    grad_heads,
    log_sum,
    delta_rows,
):
    micro, span_len, kv_heads, groups, head_dim = queries.shape
    seq_len = segments.shape[1]
    f32 = jnp.float32
    back_state = (
        jnp.zeros((kv_heads, groups, span_len, head_dim), f32),
        jnp.zeros((seq_len, kv_heads * head_dim), f32),
        jnp.zeros((seq_len, kv_heads * head_dim), f32),
    )

    def one(query_rows, key_rows, value_rows, query_seg, seg_row, grad_rows, logs, deltas):
        return attend_backward(
            back_state,
            (key_rows, value_rows),
            query_rows,
            query_pos,
            query_seg,
            seg_row,
            score_scale,
            grad_rows,
            logs,
            deltas,
        )

    return jax.vmap(one)(
        queries, keys_all, values_all, query_segs, segments, grad_heads, log_sum, delta_rows
    )


def on_device(
    hidden_in,
    segments,
    routes,
    grad_out,
    gain_attn,
    w_query,
    w_key,
    w_value,
    w_out,
    gain_moe,
    w_router,
    w_in,
    w_down,
):
    span_len = hidden_in.shape[1]
    model_width = hidden_in.shape[2]
    ctx_size = lax.axis_size("ctx")
    my_index = lax.axis_index("ctx")
    exp_dev = w_in.shape[0]
    experts = exp_dev * ctx_size
    hidden = w_down.shape[1]
    top_count = routes.shape[2]
    capacity = span_len * top_count * 5 // (4 * experts)
    kv_heads = KV_HEADS
    head_dim = HEAD_DIM
    groups = HEADS // KV_HEADS
    kv_width = kv_heads * head_dim
    seq_len = segments.shape[1]
    score_scale = head_dim ** (-0.5)
    query_pos = my_index * span_len + jnp.arange(span_len, dtype=jnp.int32)
    cosine, sine_table = rope_tables(query_pos, head_dim)
    assigns = span_len * top_count
    expert_ids = jnp.arange(experts, dtype=jnp.int32)
    f32 = jnp.float32
    bf16 = jnp.bfloat16

    micro = hidden_in.shape[0]
    rows = micro * span_len
    dp_size = lax.axis_size("dp")
    qkv_width = w_query.shape[1] + 2 * kv_width
    q_width = w_query.shape[1]
    shard_rows = w_query.shape[0]
    used_width = qkv_width + w_out.shape[1] + experts + 2
    pack_width = -(-used_width // 128) * 128

    packed = jnp.concatenate(
        [
            w_query,
            w_key,
            w_value,
            w_out,
            w_router,
            gain_attn[:, None],
            gain_moe[:, None],
            jnp.zeros((shard_rows, pack_width - used_width), bf16),
        ],
        1,
    )
    packed = lax.all_gather(packed, ("dp", "ctx"), axis=0, tiled=True)
    qkv_full = packed[:, :qkv_width]
    proj_full = packed[:, qkv_width : qkv_width + w_out.shape[1]]
    tail = qkv_width + w_out.shape[1]
    router_full = packed[:, tail : tail + experts]
    gain_one = packed[:, tail + experts].astype(f32)
    gain_two = packed[:, tail + experts + 1].astype(f32)
    in_full = lax.all_gather(w_in, "dp", axis=1, tiled=True)
    down_full = lax.all_gather(w_down, "dp", axis=2, tiled=True)

    def exchange(block):
        return lax.all_to_all(block, "ctx", split_axis=0, concat_axis=0, tiled=True)

    route_rows = routes.reshape(rows, top_count)
    chosen = (route_rows[:, :, None] == expert_ids).astype(f32)
    has = jnp.sum(chosen, 1).astype(bf16).reshape(micro, span_len, experts)
    step = jnp.arange(span_len)
    earlier = (step[None, :] < step[:, None]).astype(bf16)
    rank = jnp.einsum("tu,mue->mte", earlier, has, preferred_element_type=f32)
    which = jnp.arange(micro, dtype=f32)[:, None, None] * capacity
    rank = (rank + which).reshape(rows, 1, experts)
    slots = micro * capacity
    rank_index = jnp.sum(chosen * rank, -1).astype(jnp.int32)
    slot_index = (route_rows * slots + rank_index).reshape(rows * top_count)
    total = rows * top_count
    sources = (
        jnp.full((experts * slots,), total, jnp.int32)
        .at[slot_index]
        .set(jnp.arange(total, dtype=jnp.int32))
    )
    token_src = sources // top_count
    padded_out = jnp.concatenate(
        [grad_out.reshape(rows, model_width), jnp.zeros((1, model_width), bf16)], 0
    )
    out_rows = padded_out[token_src].reshape(ctx_size, exp_dev, slots, model_width)
    recv_out = exchange(out_rows)

    cosine = jnp.tile(cosine, (micro, 1, 1))
    sine_table = jnp.tile(sine_table, (micro, 1, 1))
    inputs = hidden_in.reshape(rows, model_width).astype(f32)
    grad_final = grad_out.reshape(rows, model_width).astype(f32)
    inverse_one = lax.rsqrt(jnp.mean(inputs * inputs, -1, keepdims=True) + EPS)
    normed_one = inputs * inverse_one
    act_in = (normed_one * gain_one).astype(bf16)
    raw = jnp.dot(act_in, qkv_full, preferred_element_type=f32)
    queries = rotate(raw[:, :q_width].reshape(rows, HEADS, head_dim), cosine, sine_table)
    queries = queries.astype(bf16).reshape(micro, span_len, kv_heads, groups, head_dim)
    keys_low = rotate(
        raw[:, q_width : q_width + kv_width].reshape(rows, kv_heads, head_dim), cosine, sine_table
    )
    keys_low = keys_low.astype(bf16).reshape(micro, span_len, kv_width)
    values_low = raw[:, q_width + kv_width :].astype(bf16).reshape(micro, span_len, kv_width)
    kv_all = lax.all_gather(
        jnp.concatenate([keys_low, values_low], -1), "ctx", axis=1, tiled=True
    )
    keys_all = kv_all[..., :kv_width]
    values_all = kv_all[..., kv_width:]
    query_segs = lax.dynamic_slice_in_dim(segments, my_index * span_len, span_len, 1)
    attn_heads, log_sum = attention_forward(
        queries, keys_all, values_all, query_pos, query_segs, segments, score_scale
    )
    attn_rows = attn_heads.transpose(0, 3, 1, 2, 4).reshape(rows, HEADS * head_dim)
    attn_low = attn_rows.astype(bf16)
    resid = inputs + jnp.einsum("th,dh->td", attn_low, proj_full, preferred_element_type=f32)
    inverse_two = lax.rsqrt(jnp.mean(resid * resid, -1, keepdims=True) + EPS)
    normed_two = resid * inverse_two
    moe_in = (normed_two * gain_two).astype(bf16)
    logits = jnp.dot(moe_in, router_full, preferred_element_type=f32)
    selected = jnp.sum(chosen * logits[:, None, :], -1)
    gate_weights = jax.nn.softmax(selected, -1)
    padded_in = jnp.concatenate([moe_in, jnp.zeros((1, model_width), bf16)], 0)
    sent_rows = padded_in[token_src].reshape(ctx_size, exp_dev, slots, model_width)
    gate_slots = (
        jnp.zeros((experts * slots,), f32)
        .at[slot_index]
        .set(gate_weights.reshape(total))
        .reshape(ctx_size, exp_dev * slots)
    )
    recv_rows = exchange(sent_rows)
    recv_gates = exchange(gate_slots).reshape(ctx_size, exp_dev, slots, 1)
    recv_grads = (recv_gates * recv_out.astype(f32)).astype(bf16)
    mixed_pre = jnp.einsum("sepd,edf->sepf", recv_rows, in_full, preferred_element_type=f32)
    gate_part = mixed_pre[..., :hidden]
    up_part = mixed_pre[..., hidden:]
    sigmoid_gate = jax.nn.sigmoid(gate_part)
    swish_gate = gate_part * sigmoid_gate
    product = (swish_gate * up_part).astype(bf16)
    result = jnp.einsum("sepf,efd->sepd", product, down_full, preferred_element_type=f32)
    returned = exchange(result.astype(bf16))
    grad_prod = jnp.einsum("sepd,efd->sepf", recv_grads, down_full, preferred_element_type=f32)
    grad_mixed = jnp.concatenate(
        [
            grad_prod * up_part * sigmoid_gate * (1.0 + gate_part * (1.0 - sigmoid_gate)),
            grad_prod * swish_gate,
        ],
        -1,
    ).astype(bf16)
    grad_rows_in = jnp.einsum("sepf,edf->sepd", grad_mixed, in_full, preferred_element_type=f32)
    grad_back = exchange(grad_rows_in.astype(bf16)).reshape(experts * slots, model_width)
    acc_down = jnp.einsum("sepf,sepd->efd", product, recv_grads, preferred_element_type=f32)
    acc_in = jnp.einsum("sepd,sepf->edf", recv_rows, grad_mixed, preferred_element_type=f32)
    grad_in = lax.psum_scatter(acc_in.astype(bf16), "dp", scatter_dimension=1, tiled=True)
    grad_down = lax.psum_scatter(acc_down.astype(bf16), "dp", scatter_dimension=2, tiled=True)

    y_slots = returned.reshape(experts * slots, model_width)
    y_tokens = y_slots[slot_index].reshape(rows, top_count, model_width)
    moe_out = jnp.sum(gate_weights[:, :, None] * y_tokens, 1)
    output_hidden = (resid + moe_out).astype(bf16)
    grad_gate = jnp.sum(grad_final[:, None, :] * y_tokens, -1)
    grad_sel = gate_weights * (grad_gate - jnp.sum(gate_weights * grad_gate, -1, keepdims=True))
    grad_logit = jnp.sum(grad_sel[:, :, None] * chosen, 1).astype(bf16)
    acc_router = jnp.einsum("td,te->de", moe_in, grad_logit, preferred_element_type=f32)
    grad_moe_in = jnp.einsum("te,de->td", grad_logit, router_full, preferred_element_type=f32)
    grad_moe_in = grad_moe_in + jnp.sum(
        grad_back[slot_index].reshape(rows, top_count, model_width), 1, dtype=f32
    )
    acc_gain_two = jnp.sum(grad_moe_in * normed_two, 0)
    grad_resid = grad_final + norm_back(grad_moe_in, normed_two, inverse_two, gain_two)
    grad_attn_in = grad_resid.astype(bf16)
    acc_proj = jnp.einsum("td,th->dh", grad_attn_in, attn_low, preferred_element_type=f32)
    grad_attn_low = jnp.dot(grad_attn_in, proj_full, preferred_element_type=f32).astype(bf16)
    grad_heads = grad_attn_low.reshape(micro, span_len, kv_heads, groups, head_dim)
    delta_rows = jnp.sum(
        (grad_attn_low * attn_rows).reshape(micro, span_len, kv_heads, groups, head_dim), -1
    ).transpose(0, 2, 3, 1)
    grad_query, grad_keys, grad_values = attention_backward(
        queries,
        keys_all,
        values_all,
        query_pos,
        query_segs,
        segments,
        score_scale,
        grad_heads,
        log_sum,
        delta_rows,
    )
    grad_kv = jnp.concatenate([grad_keys.astype(bf16), grad_values.astype(bf16)], -1)
    grad_kv = grad_kv.reshape(micro, ctx_size, span_len, 2 * kv_width).transpose(1, 0, 2, 3)
    grad_kv = jnp.sum(exchange(grad_kv), 0, dtype=f32).reshape(rows, 2 * kv_width)
    query_turn = grad_query.transpose(0, 3, 1, 2, 4).reshape(rows, HEADS, head_dim)
    grad_q_raw = rotate_back(query_turn, cosine, sine_table).reshape(rows, q_width)
    grad_k_raw = rotate_back(
        grad_kv[:, :kv_width].reshape(rows, kv_heads, head_dim), cosine, sine_table
    ).reshape(rows, kv_width)
    grad_raw = jnp.concatenate(
        [grad_q_raw.astype(bf16), grad_k_raw.astype(bf16), grad_kv[:, kv_width:].astype(bf16)], 1
    )
    acc_qkv = jnp.einsum("td,th->dh", act_in, grad_raw, preferred_element_type=f32)
    grad_act = jnp.einsum("th,dh->td", grad_raw, qkv_full, preferred_element_type=f32)
    acc_gain_one = jnp.sum(grad_act * normed_one, 0)
    grad_hidden = grad_resid + norm_back(grad_act, normed_one, inverse_one, gain_one)

    def reduce_rows(block):
        width = block.shape[1]
        halves = block.reshape(dp_size, ctx_size * shard_rows, width)
        if dp_size == 2:
            mine = lax.axis_index("dp")
            away = lax.dynamic_index_in_dim(halves, 1 - mine, 0, keepdims=False).astype(bf16)
            got = lax.ppermute(away, "dp", [(0, 1), (1, 0)])
            half = lax.dynamic_index_in_dim(halves, mine, 0, keepdims=False) + got.astype(f32)
        else:
            half = lax.psum_scatter(halves, "dp", scatter_dimension=0, tiled=False)
        parts = exchange(half.astype(bf16).reshape(ctx_size, shard_rows, width))
        return jnp.sum(parts, 0, dtype=f32)

    early = reduce_rows(
        jnp.concatenate(
            [
                acc_proj,
                acc_router,
                acc_gain_two[:, None],
                jnp.zeros((model_width, 127 - experts % 128), f32),
            ],
            1,
        )
    )
    late = reduce_rows(
        jnp.concatenate([acc_qkv, acc_gain_one[:, None], jnp.zeros((model_width, 127), f32)], 1)
    )
    proj_width = w_out.shape[1]
    return (
        output_hidden.reshape(micro, span_len, model_width),
        grad_hidden.reshape(micro, span_len, model_width),
        late[:, qkv_width],
        late[:, :q_width],
        late[:, q_width : q_width + kv_width],
        late[:, q_width + kv_width : qkv_width],
        early[:, :proj_width],
        early[:, proj_width + experts],
        early[:, proj_width : proj_width + experts],
        grad_in.astype(f32),
        grad_down.astype(f32),
    )


def solution(mesh):
    placed = (
        P("dp", "ctx", None),
        P("dp", None),
        P("dp", "ctx", None),
        P("dp", "ctx", None),
        P(("dp", "ctx")),
        P(("dp", "ctx"), None),
        P(("dp", "ctx"), None),
        P(("dp", "ctx"), None),
        P(("dp", "ctx"), None),
        P(("dp", "ctx")),
        P(("dp", "ctx"), None),
        P("ctx", "dp", None),
        P("ctx", None, "dp"),
    )
    return jax.shard_map(
        on_device,
        mesh=mesh,
        in_specs=placed,
        out_specs=(
            P("dp", "ctx", None),
            P("dp", "ctx", None),
            P(("dp", "ctx")),
            P(("dp", "ctx"), None),
            P(("dp", "ctx"), None),
            P(("dp", "ctx"), None),
            P(("dp", "ctx"), None),
            P(("dp", "ctx")),
            P(("dp", "ctx"), None),
            P("ctx", "dp", None),
            P("ctx", None, "dp"),
        ),
        check_vma=False,
    )
```

time: 2510 us -> 1480 us (0.59)
  waiting for transfers between devices: 1430 us -> 760 us
  blocking collectives: 411 us -> 0 us
  starting transfers between devices: 85.2 us -> 156 us
  matrix products: 238 us -> 180 us
  local copies, waits for them, and re-layouts: 201 us -> 253 us
    reduce_scatter x11 -> x2, waiting for transfers between devices: 787 us -> 0.03 us  [the longest x1 0.03 us: on_device(): lax.psum_scatter(acc_down.astype(bf16), 'dp', scatter_dimension=2, tiled=...]
    all_to_all x8, waiting for transfers between devices: 199 us -> 468 us  [exchange(): return lax.all_to_all(block, 'ctx', split_axis=0, concat_axis=0, tiled=True)]
    all_gather x3 -> x0, blocking collectives: 250 us -> none  [gather_layer(): lax.all_gather(shards[6], ('dp', 'ctx'), axis=0, tiled=True)]
    unnamed x3 -> x0, blocking collectives: 162 us -> none
    all_gather x22 -> x4, waiting for transfers between devices: 435 us -> 291 us  [the longest x1 201 us: on_device(): lax.all_gather(jnp.concatenate([keys_low, values_low], -1), 'ctx', axis=1...]
    all_to_all x8, starting transfers between devices: 82.1 us -> 155 us  [exchange(): return lax.all_to_all(block, 'ctx', split_axis=0, concat_axis=0, tiled=True)]
    slice x5 -> x17, local copies, waits for them, and re-layouts: 0.43 us -> 39.5 us  [the longest x2 19.7 us: on_device(): values_all = kv_all[..., kv_width:]]
    dot_general x20 -> x4, matrix products: 45.1 us -> 12.7 us  [the longest x1 4.7 us: on_device(): jnp.einsum('th,dh->td', grad_raw, qkv_full, preferred_element_type=f32)]
  transfers between devices with their start and end apart: 41 -> 16, of which waited for: 26 -> 11; matrix products, arithmetic and copies ran while one was open for 15% -> 13% of each run, Pallas kernels for 0% -> 0%
where the time goes in v1:
time: 1480 us; the launch traced here: 1470 us
  waiting for transfers between devices  760 us (51%)
  local copies, waits for them, and re-layouts  253 us (17%)
  matrix products  180 us (12%)
  starting transfers between devices  156 us (11%)
  other arithmetic  87.6 us (6%)
  between operations  17 us (1%)
  loops' own time  16.3 us (1%)
    all_to_all x8, waiting for transfers between devices, exchange(): return lax.all_to_all(block, 'ctx', split_axis=0, concat_axis=0, tiled=True)  468 us
    all_gather x1, waiting for transfers between devices, on_device(): lax.all_gather(jnp.concatenate([keys_low, values_low], -1), 'ctx', axis=1...  201 us
    all_to_all x8, starting transfers between devices, exchange(): return lax.all_to_all(block, 'ctx', split_axis=0, concat_axis=0, tiled=True)  155 us
    all_gather x1, waiting for transfers between devices, on_device(): packed = lax.all_gather(packed, ('dp', 'ctx'), axis=0, tiled=True)  72.4 us
  transfers between devices with their start and end apart: 16, of which 11 were waited for; matrix products, arithmetic and copies ran while one was open for 13% of the time, Pallas kernels for 0%

profile of v1, /device:TPU:0, one launch (start us, length us, event | category | flops | bytes accessed | tf_op | source)
XLA Modules:
  0.0 1469.9 jit_solution(7746874905625311178)
XLA Ops:
  13.2 72.4 %all-gather.5.cloned.1.call-done = bf16[1024,3200]{1,0:T(8,128)(2,1)} async-done(((bf16[32,3200]{1,0:T(8,128)(2,1)}), bf16[1024,3200]{1,0:T(8,128)(2,1)}) %all-gather.5.cloned.1.call-update) | async-done | bytes 6553616 | tf_op jit(solution)/shard_map/all_gather | solution.py:275
  101.1 201.3 %all-gather.7.cloned.1.call-done = bf16[2,2048,1024]{1,0,2:T(2,128)(2,1)} async-done(((bf16[2,128,1024]{1,0,2:T(2,128)(2,1)}), bf16[2,2048,1024]{1,0,2:T(2,128)(2,1)}) %all-gather.7.cloned.1.call-update) | async-done | bytes 8388624 | tf_op jit(solution)/shard_map/all_gather | solution.py:327
  302.4 8.6 fusion.110
  311.0 11.2 copy.212
  322.1 7.3 copy.216
  329.4 11.1 copy.215
  340.5 7.3 copy.218
  347.8 77.6 %while.32 = (s32[]{:T(128)}, f32[2,8,2,128]{3,2,1,0:T(2,128)S(1)}, f32[2,8,2,128]{3,2,1,0:T(2,128)S(1)}, f32[2,8,2,128,64]{3,4,2,1,0:T(8,128)}, s32[4]{0:T(128)S...) while((s32[]{:T(128)}, f32[2,8,2,128]{3,2,1,0:T(2,128)S(1)}, ...), condition=%wide.region_4.5_spmd.clone, body=%wide.region_1.4_spmd.clone.sunk | while | flops 561074816 | bytes 68569320 | solution.py:87
  353.1 4.7 fusion.168
  357.8 5.3 fusion.170
  371.6 4.7 fusion.168
  376.3 5.3 fusion.170
  382.0 3.9 fusion.172
  391.3 4.7 fusion.168
  396.0 5.3 fusion.170
  411.0 4.7 fusion.168
  415.7 5.3 fusion.170
  433.6 8.1 scatter_custom_fusion.1
  442.3 5.5 all-to-all-start.2
  447.9 8.1 scatter_custom_fusion
  456.0 9.3 gather_fusion
  465.4 7.1 all-to-all-start
  472.5 8.8 gather_fusion.2
  481.4 87.3 %all-to-all-done = bf16[16,2,80,1024]{3,2,1,0:T(8,128)(2,1)} async-done(((bf16[16,2,80,1024]{3,2,1,0:T(8,128)(2,1)}), bf16[16,2,80,1024]{3,2,1,0:T(8,128)(2,1)}, u32[]{:S(2)}, u32[]{:S(2)}) %all-to-all-start) | async-done | bytes 5242912 | tf_op jit(solution)/shard_map/all_to_all | solution.py:286
  568.7 23.6 %all-to-all-start.3 = ((bf16[16,2,80,1024]{3,2,1,0:T(8,128)(2,1)}), bf16[16,2,80,1024]{3,2,1,0:T(8,128)(2,1)}, u32[]{:S(2)}, u32[]{:S(2)}) async-start(bf16[16,2,80,1024]{3,2,1,0:T(8,128)(2,1)} %bitcast.341), calls=%async_computation.3 | async-start | bytes 10485760 | tf_op jit(solution)/shard_map/all_to_all | solution.py:286
  593.6 15.5 %all-gather.9.cloned.1.call-done = bf16[2,1024,1024]{2,1,0:T(8,128)(2,1)} async-done(((bf16[2,512,1024]{2,1,0:T(8,128)(2,1)}), bf16[2,1024,1024]{2,1,0:T(8,128)(2,1)}) %all-gather.9.cloned.1.call-update) | async-done | bytes 4194320 | tf_op jit(solution)/shard_map/all_gather | solution.py:282
  609.1 11.2 fusion.52
  622.2 67.1 %all-to-all-done.3 = bf16[16,2,80,1024]{3,2,1,0:T(8,128)(2,1)} async-done(((bf16[16,2,80,1024]{3,2,1,0:T(8,128)(2,1)}), bf16[16,2,80,1024]{3,2,1,0:T(8,128)(2,1)}, u32[]{:S(2)}, u32[]{:S(2)}) %all-to-all-start.3) | async-done | bytes 5242912 | tf_op jit(solution)/shard_map/all_to_all | solution.py:286
  689.3 10.9 fusion.37
  706.4 24.0 %all-to-all-start.1 = ((bf16[16,2,80,1024]{3,2,1,0:T(8,128)(2,1)}), bf16[16,2,80,1024]{3,2,1,0:T(8,128)(2,1)}, u32[]{:S(2)}, u32[]{:S(2)}) async-start(bf16[16,2,80,1024]{3,2,1,0:T(8,128)(2,1)} %copy.226), calls=%async_computation.1 | async-start | bytes 10485760 | tf_op jit(solution)/shard_map/all_to_all | solution.py:286
  730.4 8.9 convert_bitcast_fusion
  742.3 85.1 %all-to-all-done.1 = bf16[16,2,80,1024]{3,2,1,0:T(8,128)(2,1)} async-done(((bf16[16,2,80,1024]{3,2,1,0:T(8,128)(2,1)}), bf16[16,2,80,1024]{3,2,1,0:T(8,128)(2,1)}, u32[]{:S(2)}, u32[]{:S(2)}) %all-to-all-start.1) | async-done | bytes 5242912 | tf_op jit(solution)/shard_map/all_to_all | solution.py:286
  827.4 24.2 %all-to-all-start.4 = ((bf16[16,2,80,1024]{3,2,1,0:T(8,128)(2,1)}), bf16[16,2,80,1024]{3,2,1,0:T(8,128)(2,1)}, u32[]{:S(2)}, u32[]{:S(2)}) async-start(bf16[16,2,80,1024]{3,2,1,0:T(8,128)(2,1)} %copy.231), calls=%async_computation.4 | async-start | bytes 10485760 | tf_op jit(solution)/shard_map/all_to_all | solution.py:286
  857.5 14.1 gather_fusion.1
  871.6 6.2 fusion.34
  878.0 70.5 %all-to-all-done.4 = bf16[16,2,80,1024]{3,2,1,0:T(8,128)(2,1)} async-done(((bf16[16,2,80,1024]{3,2,1,0:T(8,128)(2,1)}), bf16[16,2,80,1024]{3,2,1,0:T(8,128)(2,1)}, u32[]{:S(2)}, u32[]{:S(2)}) %all-to-all-start.4) | async-done | bytes 5242912 | tf_op jit(solution)/shard_map/all_to_all | solution.py:286
  948.5 14.1 gather_fusion.3
  962.6 5.5 convert_reduce_fusion.1
  977.3 129.9 %while.33 = (s32[]{:T(128)}, f32[2,8,2,128,64]{3,4,2,1,0:T(8,128)}, bf16[4,2,512,512]{3,2,0,1:T(8,128)(2,1)}, bf16[4,2,512,512]{3,2,0,1:T(8,128)(2,1)}, s32[4]{0...) while((s32[]{:T(128)}, f32[2,8,2,128,64]{3,4,2,1,0:T(8,128)}, ...), condition=%wide.region_21.22_spmd.clone, body=%wide.region_20.21_spmd.clone.sunk | while | flops 1365312128 | bytes 110693144 | solution.py:141
  994.7 6.0 fusion.186
  1005.8 3.9 fusion.185
  1026.9 6.0 fusion.186
  1037.9 4.2 fusion.185
  1059.4 6.0 fusion.186
  1070.4 4.2 fusion.185
  1091.9 6.0 fusion.186
  1102.9 4.2 fusion.185
  1107.2 8.1 maximum_bitcast_fusion
  1115.2 8.2 copy.247
  1123.4 24.2 %all-to-all-start.5 = ((bf16[16,2,128,1024]{3,2,1,0:T(8,128)(2,1)}), bf16[16,2,128,1024]{3,2,1,0:T(8,128)(2,1)}, u32[]{:S(2)}, u32[]{:S(2)}) async-start(bf16[16,2,128,1024]{3,2,1,0:T(8,128)(2,1)} %copy.247), calls=%async_computation.5 | async-start | bytes 16777216 | tf_op jit(solution)/shard_map/all_to_all | solution.py:286
  1147.7 6.8 bitcast_convert_fusion.1
  1160.3 11.3 bitcast_convert_fusion
  1184.3 6.6 concatenate.85
  1202.1 100.1 %all-to-all-done.5 = bf16[16,2,128,1024]{3,2,1,0:T(8,128)(2,1)} async-done(((bf16[16,2,128,1024]{3,2,1,0:T(8,128)(2,1)}), bf16[16,2,128,1024]{3,2,1,0:T(8,128)(2,1)}, u32[]{:S(2)}, u32[]{:S(2)}) %all-to-all-start.5) | async-done | bytes 8388640 | tf_op jit(solution)/shard_map/all_to_all | solution.py:286
  1302.2 5.5 convert_reduce_fusion
  1313.0 4.7 multiply_reduce_fusion.1
  1318.0 4.5 fusion.85
  1322.6 10.2 concatenate.82
  1339.8 39.5 %all-to-all-start.7 = ((bf16[16,32,1152]{2,1,0:T(8,128)(2,1)}), bf16[16,32,1152]{2,1,0:T(8,128)(2,1)S(1)}, u32[]{:S(2)}, u32[]{:S(2)}) async-start(bf16[16,32,1152]{2,1,0:T(8,128)(2,1)} %bitcast.63), calls=%async_computation.7 | async-start | bytes 2359296 | tf_op jit(solution)/shard_map/all_to_all | solution.py:286
  1379.3 4.0 fusion.48
  1383.4 23.3 %all-to-all-done.7 = bf16[16,32,1152]{2,1,0:T(8,128)(2,1)S(1)} async-done(((bf16[16,32,1152]{2,1,0:T(8,128)(2,1)}), bf16[16,32,1152]{2,1,0:T(8,128)(2,1)S(1)}, u32[]{:S(2)}, u32[]{:S(2)}) %all-to-all-start.7) | async-done | bytes 1179680 | tf_op jit(solution)/shard_map/all_to_all | solution.py:286
  1407.7 7.0 all-to-all-start.6
  1417.7 4.2 convert_element_type.283
  1425.3 34.5 %all-to-all-done.6 = bf16[16,32,2176]{2,1,0:T(8,128)(2,1)S(1)} async-done(((bf16[16,32,2176]{2,1,0:T(8,128)(2,1)}), bf16[16,32,2176]{2,1,0:T(8,128)(2,1)S(1)}, u32[]{:S(2)}, u32[]{:S(2)}) %all-to-all-start.6) | async-done | bytes 2228256 | tf_op jit(solution)/shard_map/all_to_all | solution.py:286
  (363 shorter events, 215.0 us)
Async XLA Ops:
  8.0 77.6 %all-gather.5.cloned.1.call-start = ((), (), s32[]{:S(2)}) async-start(), calls=%async_computation.10 | async-start | bytes 6758400 | tf_op jit(solution)/shard_map/all_gather | solution.py:275
  11.2 291.1 %all-gather.7.cloned.1.call-start = ((), (), s32[]{:S(2)}) async-start(), calls=%async_computation.11 | async-start | bytes 8912896 | tf_op jit(solution)/shard_map/all_gather | solution.py:327
  11.5 82.6 %copy-start.25 = (f32[8,8,2,128]{3,1,2,0:T(8,128)}, f32[8,8,2,128]{3,1,2,0:T(8,128)S(1)}, u32[]{:S(2)}) copy-start(f32[8,8,2,128]{3,1,2,0:T(8,128)S(1)} %copy.340) | copy-start | bytes 196612
  11.6 75.4 %copy-start.29 = (f32[8,8,2,128]{3,1,2,0:T(8,128)}, f32[8,8,2,128]{3,1,2,0:T(8,128)S(1)}, u32[]{:S(2)}) copy-start(f32[8,8,2,128]{3,1,2,0:T(8,128)S(1)} %copy.341) | copy-start | bytes 196612
  11.6 80.9 %copy-start.10 = (f32[256,8,64]{0,2,1:T(8,128)}, f32[256,8,64]{0,2,1:T(8,128)S(1)}, u32[]{:S(2)}) copy-start(f32[256,8,64]{0,2,1:T(8,128)S(1)} %mul.354) | copy-start | bytes 1572868
  13.2 80.7 %copy-start.37 = (f32[256]{0:T(256)}, f32[256]{0:T(256)S(1)}, u32[]{:S(2)}) copy-start(f32[256]{0:T(256)S(1)} %rsqrt_bitcast_fusion) | copy-start | bytes 3076
  87.0 7.1 copy-start.33
  92.5 1.3 copy-start.24
  92.5 4.3 copy-start.31
  93.8 3.5 copy-start.32
  347.8 80.6 %copy-start.12 = (bf16[2,128,1024]{2,1,0:T(8,128)(2,1)S(1)}, bf16[2,128,1024]{2,1,0:T(8,128)(2,1)}, u32[]{:S(2)}) copy-start(bf16[2,128,1024]{2,1,0:T(8,128)(2,1)} %param.17) | copy-start | bytes 1572868
  357.8 5.8 copy-start
  376.3 5.8 copy-start
  396.0 5.8 copy-start
  415.7 5.8 copy-start
  428.4 2.9 copy-start.15
  431.5 33.9 %copy-start.6 = (bf16[256,1024]{1,0:T(8,128)(2,1)}, bf16[256,1024]{1,0:T(8,128)(2,1)S(1)}, u32[]{:S(2)}) copy-start(bf16[256,1024]{1,0:T(8,128)(2,1)S(1)} %multiply_convert_fusion.2) | copy-start | bytes 1572868
  442.3 23.0 %all-to-all-start.2 = ((f32[16,1,160]{2,1,0:T(1,128)}), f32[16,1,160]{2,1,0:T(1,128)S(1)}, u32[]{:S(2)}, u32[]{:S(2)}) async-start(f32[16,1,160]{2,1,0:T(1,128)} %all_to_all.29), calls=%async_computation.2 | async-start | bytes 32768 | tf_op jit(solution)/shard_map/all_to_all | solution.py:286
  465.3 7.1 copy-start.7
  465.4 103.3 %all-to-all-start = ((bf16[16,2,80,1024]{3,2,1,0:T(8,128)(2,1)}), bf16[16,2,80,1024]{3,2,1,0:T(8,128)(2,1)}, u32[]{:S(2)}, u32[]{:S(2)}) async-start(bf16[16,2,80,1024]{3,2,1,0:T(8,128)(2,1)} %bitcast.342), calls=%async_computation | async-start | bytes 10485760 | tf_op jit(solution)/shard_map/all_to_all | solution.py:286
  568.7 120.6 %all-to-all-start.3 = ((bf16[16,2,80,1024]{3,2,1,0:T(8,128)(2,1)}), bf16[16,2,80,1024]{3,2,1,0:T(8,128)(2,1)}, u32[]{:S(2)}, u32[]{:S(2)}) async-start(bf16[16,2,80,1024]{3,2,1,0:T(8,128)(2,1)} %bitcast.341), calls=%async_computation.3 | async-start | bytes 10485760 | tf_op jit(solution)/shard_map/all_to_all | solution.py:286
  592.3 16.8 %all-gather.9.cloned.1.call-start = ((), (), s32[]{:S(2)}) async-start(), calls=%async_computation.12 | async-start | bytes 6291456 | tf_op jit(solution)/shard_map/all_gather | solution.py:282
  592.8 29.4 %all-gather.11.cloned.1.call-start = ((), (), s32[]{:S(2)}) async-start(), calls=%async_computation.13 | async-start | bytes 3145728 | tf_op jit(solution)/shard_map/all_gather | solution.py:283
  593.6 95.8 %copy-start.35 = (f32[16,2,80]{2,1,0:T(2,128)}, f32[16,2,80]{2,1,0:T(2,128)S(1)}, u32[]{:S(2)}) copy-start(f32[16,2,80]{2,1,0:T(2,128)S(1)} %mul.388) | copy-start | bytes 30724
  689.3 10.9 copy-start.39
  700.2 3.1 copy-start.40
  706.4 120.9 %all-to-all-start.1 = ((bf16[16,2,80,1024]{3,2,1,0:T(8,128)(2,1)}), bf16[16,2,80,1024]{3,2,1,0:T(8,128)(2,1)}, u32[]{:S(2)}, u32[]{:S(2)}) async-start(bf16[16,2,80,1024]{3,2,1,0:T(8,128)(2,1)} %copy.226), calls=%async_computation.1 | async-start | bytes 10485760 | tf_op jit(solution)/shard_map/all_to_all | solution.py:286
  827.4 121.1 %all-to-all-start.4 = ((bf16[16,2,80,1024]{3,2,1,0:T(8,128)(2,1)}), bf16[16,2,80,1024]{3,2,1,0:T(8,128)(2,1)}, u32[]{:S(2)}, u32[]{:S(2)}) async-start(bf16[16,2,80,1024]{3,2,1,0:T(8,128)(2,1)} %copy.231), calls=%async_computation.4 | async-start | bytes 10485760 | tf_op jit(solution)/shard_map/all_to_all | solution.py:286
  962.6 7.1 copy-start.16
  968.1 4.0 copy-start.18
  983.7 5.1 copy-start.2
  988.9 2.0 copy-start.1
  1015.9 5.1 copy-start.2
  1021.0 2.0 copy-start.1
  1048.4 5.1 copy-start.2
  1053.5 2.0 copy-start.1
  1080.9 5.1 copy-start.2
  1086.0 2.0 copy-start.1
  1123.4 24.3 %copy-start.36 = (f32[16,2,80]{2,1,0:T(2,128)S(1)}, f32[16,2,80]{2,1,0:T(2,128)}, u32[]{:S(2)}) copy-start(f32[16,2,80]{2,1,0:T(2,128)} %copy-done.35) | copy-start | bytes 30724
  1123.4 24.3 %copy-start.41 = (bf16[16,2,80,512]{3,2,0,1:T(8,128)(2,1)S(1)}, bf16[16,2,80,512]{3,2,0,1:T(8,128)(2,1)}, u32[]{:S(2)}) copy-start(bf16[16,2,80,512]{3,2,0,1:T(8,128)(2,1)} %copy-done.40) | copy-start | bytes 7864324
  1123.4 178.8 %all-to-all-start.5 = ((bf16[16,2,128,1024]{3,2,1,0:T(8,128)(2,1)}), bf16[16,2,128,1024]{3,2,1,0:T(8,128)(2,1)}, u32[]{:S(2)}, u32[]{:S(2)}) async-start(bf16[16,2,128,1024]{3,2,1,0:T(8,128)(2,1)} %copy.247), calls=%async_computation.5 | async-start | bytes 16777216 | tf_op jit(solution)/shard_map/all_to_all | solution.py:286
  1147.7 7.4 copy-start.30
  1147.7 267.1 %reduce-scatter.5.cloned.1.call-start = ((), (), s32[]{:S(2)}) async-start(), calls=%async_computation.15 | async-start | bytes 3145728 | tf_op jit(solution)/shard_map/reduce_scatter | solution.py:377
  1154.6 1.9 copy-start.11
  1154.6 2.9 copy-start.23
  1154.6 4.0 copy-start.19
  1154.6 263.0 %reduce-scatter.3.cloned.1.call-start = ((), (), s32[]{:S(2)}) async-start(), calls=%async_computation.14 | async-start | bytes 6291456 | tf_op jit(solution)/shard_map/reduce_scatter | solution.py:376
  1160.3 11.3 copy-start.3
  1184.3 9.4 copy-start.17
  1184.3 11.2 copy-start.26
  1193.7 142.9 %collective-permute-start.1 = (bf16[512,1152]{1,0:T(8,128)(2,1)}, bf16[512,1152]{1,0:T(8,128)(2,1)}, u32[]{:S(2)}, u32[]{:S(2)}) collective-permute-start(bf16[512,1152]{1,0:T(8,128)(2,1)} %fusion.81), channel_id=1, source_target_pairs={{0,16},{16,0},{1,17},{17,1},{2,18},{18,2},{3,19},{19,3},{4,20},{20... | collective-permute-start | bytes 3538952 | tf_op jit(solution)/shard_map/ppermute | solution.py:434
  1307.7 5.0 copy-start.21
  1307.7 5.2 copy-start.13
  1307.7 5.2 copy-start.34
  1307.7 5.2 copy-start.38
  1312.9 5.1 copy-start.20
  1312.9 5.1 copy-start.27
  1336.6 42.7 %collective-permute-start = (bf16[512,2176]{1,0:T(8,128)(2,1)}, bf16[512,2176]{1,0:T(8,128)(2,1)S(1)}, u32[]{:S(2)}, u32[]{:S(2)}) collective-permute-start(bf16[512,2176]{1,0:T(8,128)(2,1)} %fusion.66), channel_id=1, source_target_pairs={{0,16},{16,0},{1,17},{17,1},{2,18},{18,2},{3,19},{19,3},{4,20},{20... | collective-permute-start | bytes 6684680 | tf_op jit(solution)/shard_map/ppermute | solution.py:434
  1339.8 66.8 %all-to-all-start.7 = ((bf16[16,32,1152]{2,1,0:T(8,128)(2,1)}), bf16[16,32,1152]{2,1,0:T(8,128)(2,1)S(1)}, u32[]{:S(2)}, u32[]{:S(2)}) async-start(bf16[16,32,1152]{2,1,0:T(8,128)(2,1)} %bitcast.63), calls=%async_computation.7 | async-start | bytes 2359296 | tf_op jit(solution)/shard_map/all_to_all | solution.py:286
  1407.7 52.1 %all-to-all-start.6 = ((bf16[16,32,2176]{2,1,0:T(8,128)(2,1)}), bf16[16,32,2176]{2,1,0:T(8,128)(2,1)S(1)}, u32[]{:S(2)}, u32[]{:S(2)}) async-start(bf16[16,32,2176]{2,1,0:T(8,128)(2,1)} %bitcast.57), calls=%async_computation.6 | async-start | bytes 4456448 | tf_op jit(solution)/shard_map/all_to_all | solution.py:286
  1414.7 9.3 copy-start.5
  1417.7 4.2 copy-start.9
  1417.7 6.4 copy-start.14
  1417.7 6.4 copy-start.28
  (3 other events, 2.8 us)
Sparse Core Ops, SparseCore 0:
  12.3 73.2 all-gather.4
  96.9 205.4 all-gather.6
Sparse Core Ops, SparseCore 1:
  594.3 14.8 all-gather.8
  610.5 11.6 all-gather.10
  1154.7 10.8 reduce-scatter.4
  1171.7 13.2 reduce-scatter.2
